TPU v7x, 32 devices: a whole 2x2x4 slice. The times are simulated.
32 devices in a mesh: image: 2 (over x), orb: 16 (over z, y, core).
Axes of the slice: x: 2, y: 2, z: 4, core: 2. Of those that a mesh axis runs over, the one named last changes fastest.
Arguments:
- orb_blocks: bfloat16 [128, 256, 512], P(('image', 'orb')), parts along dimension 0, may hold values from -6 to 6
- pno: bfloat16 [1536, 200, 256], P(('image', 'orb')), parts along dimension 0, may hold values from -0.375 to 0.375
- pno_levels: float32 [1536, 200], P(('image', 'orb')), parts along dimension 0, may hold values from 0.5 to 4
- occ_levels: float32 [128], P(('image', 'orb')), parts along dimension 0, may hold values from -1.5 to -0.3
- pair_i_local: int32 [1536], P(('image', 'orb')), parts along dimension 0, may hold values from 0 to 3
- fetch_local: int32 [1024], P(('image', 'orb')), parts along dimension 0, may hold values from 0 to 3, as said below
- pair_slot: int32 [1536, 1], P(('image', 'orb')), parts along dimension 0, may hold values from 0 to 31; in each aligned block of 48 rows (0 to 47, 48 to 95, ...) at most 3 rows name the same one
Outputs:
- amplitudes: float32 [1536, 200, 200], P(('image', 'orb')), parts along dimension 0
- density: float32 [128, 256, 512], P(('image', 'orb')), parts along dimension 0
There are 2 independent parts, one for each index of `image`. A program takes and returns all parts, laid end to end along the dimension named above; each array names one. Nothing has to cross between parts.
Inputs may be any that keep to these rules, and one draw needn't show every extreme that they name: `pair_slot`: within the 48 pairs of one device, no slot is named by more than 3 pairs; in some devices one slot is named by exactly 3. `fetch_local`: the 2 orbitals that one device asks of one owner are distinct.
All inputs are finite; a program needn't handle non-finite values.
Results may differ from a plain program's by a relative error of at most 0.0037.
Values may be sent and summed in bfloat16 or wider, within the bound.
A program may use at most 192 MiB of HBM per device.

v0:
```python
import jax
import jax.numpy as jnp
from jax import lax
from jax.sharding import PartitionSpec as P

MOST = 3
ITERS = 2


shift_weight = 0.1


def on_device(orb_blocks, pno, pno_levels, occ_levels, pair_i_local, fetch_local, pair_slot):
    orb_count = orb_blocks.shape[0]
    pair_count = pno.shape[0]
    pno_width = pno.shape[1]
    aux_width = orb_blocks.shape[2]
    slot_total = fetch_local.shape[0]
    per_owner = slot_total // lax.axis_size("orb")
    own_index = lax.axis_index("orb")
    slot_of = pair_slot[:, 0]
    pair_ids = jnp.arange(pair_count, dtype=jnp.int32)
    slot_ids = jnp.arange(slot_total, dtype=jnp.int32)
    asked = lax.all_to_all(fetch_local, "orb", split_axis=0, concat_axis=0, tiled=True)
    levels = lax.all_gather(occ_levels, "orb", axis=0, tiled=True)
    reply = jnp.take(orb_blocks, asked, axis=0)
    fetched = lax.all_to_all(reply, "orb", split_axis=0, concat_axis=0, tiled=True)
    slot_orb = slot_ids // per_owner * orb_count + fetch_local
    pair_in_slot = slot_of[:, None] == slot_ids[None, :]
    first_orb = own_index * orb_count + pair_i_local
    second_orb = jnp.sum(jnp.where(pair_in_slot, slot_orb[None, :], 0), axis=1)
    orb_ids = jnp.arange(levels.shape[0], dtype=jnp.int32)
    first_hot = first_orb[:, None] == orb_ids[None, :]
    second_hot = second_orb[:, None] == orb_ids[None, :]
    zero_half = jnp.zeros((), jnp.bfloat16)
    first_blocks = jnp.take(orb_blocks, pair_i_local, axis=0)
    first_proj = jnp.einsum(
        "pav,pvx->pax", pno, first_blocks, preferred_element_type=jnp.float32
    ).astype(jnp.bfloat16)
    second_blocks = jnp.take(fetched, slot_of, axis=0)
    second_proj = jnp.einsum(
        "pav,pvx->pax", pno, second_blocks, preferred_element_type=jnp.float32
    ).astype(jnp.bfloat16)
    coulomb = jnp.einsum(
        "pax,pbx->pab", first_proj, second_proj, preferred_element_type=jnp.float32
    ) * aux_width ** (-0.5)
    first_level = jnp.sum(jnp.where(first_hot, levels[None, :], 0.0), axis=1)
    second_level = jnp.sum(jnp.where(second_hot, levels[None, :], 0.0), axis=1)
    denominator = (
        pno_levels[:, :, None]
        + pno_levels[:, None, :]
        - (first_level + second_level)[:, None, None]
    )
    amplitude = -coulomb / denominator
    for sweep in range(ITERS):
        pair_energy = jnp.sum(
            coulomb * (2.0 * amplitude - jnp.swapaxes(amplitude, 1, 2)), axis=(1, 2)
        ) / (pno_width * pno_width)
        partial_energy = jnp.sum(jnp.where(first_hot, pair_energy[:, None], 0.0), axis=0) + jnp.sum(
            jnp.where(second_hot, pair_energy[:, None], 0.0), axis=0
        )
        shifts = shift_weight * lax.psum(partial_energy, "orb")
        pair_shift = jnp.sum(jnp.where(first_hot, shifts[None, :], 0.0), axis=1) + jnp.sum(
            jnp.where(second_hot, shifts[None, :], 0.0), axis=1
        )
        residual = coulomb + (denominator + pair_shift[:, None, None]) * amplitude
        amplitude = amplitude - residual / denominator
    amp_half = amplitude.astype(jnp.bfloat16)
    first_part = jnp.einsum(
        "pab,pbx->pax", amp_half, second_proj, preferred_element_type=jnp.float32
    ).astype(jnp.bfloat16)
    second_part = jnp.einsum(
        "pba,pbx->pax", amp_half, first_proj, preferred_element_type=jnp.float32
    ).astype(jnp.bfloat16)
    first_pao = jnp.einsum(
        "pav,pax->pvx", pno, first_part, preferred_element_type=jnp.float32
    ).astype(jnp.bfloat16)
    second_pao = jnp.einsum(
        "pav,pax->pvx", pno, second_part, preferred_element_type=jnp.float32
    ).astype(jnp.bfloat16)
    local_ids = jnp.arange(orb_count, dtype=jnp.int32)
    pair_hot = (pair_i_local[None, :] == local_ids[:, None]).astype(jnp.bfloat16)
    density = jnp.einsum("op,pvx->ovx", pair_hot, first_pao, preferred_element_type=jnp.float32)
    earlier = (slot_of[:, None] == slot_of[None, :]) & (pair_ids[None, :] < pair_ids[:, None])
    row_of = slot_of * MOST + jnp.sum(earlier.astype(jnp.int32), axis=1)
    row_ids = jnp.arange(slot_total * MOST, dtype=jnp.int32)
    placed = row_ids[:, None] == row_of[None, :]
    filled = jnp.any(placed, axis=1)
    row_pair = jnp.sum(jnp.where(placed, pair_ids[None, :], 0), axis=1)
    sending = jnp.where(filled[:, None, None], jnp.take(second_pao, row_pair, axis=0), zero_half)
    home_terms = lax.all_to_all(sending, "orb", split_axis=0, concat_axis=0, tiled=True)
    home_orb = jnp.repeat(asked, MOST)
    home_hot = (home_orb[None, :] == local_ids[:, None]).astype(jnp.bfloat16)
    density = density + jnp.einsum(
        "or,rvx->ovx", home_hot, home_terms, preferred_element_type=jnp.float32
    )
    return (amplitude, density)


def solution(mesh):
    placed = (
        P(("image", "orb"), None, None),
        P(("image", "orb"), None, None),
        P(("image", "orb"), None),
        P(("image", "orb")),
        P(("image", "orb")),
        P(("image", "orb")),
        P(("image", "orb"), None),
    )
    return jax.shard_map(
        on_device,
        mesh=mesh,
        in_specs=placed,
        out_specs=(P(("image", "orb"), None, None), P(("image", "orb"), None, None)),
        check_vma=False,
    )
```

profile of v0, /device:TPU:15, one launch (start us, length us, event | category | flops | bytes accessed | tf_op | source)
XLA Modules:
  0.0 1022.4 jit_solution(8251008075074752223)
XLA Ops:
  1.5 10.2 all_to_all.25
  18.1 7.7 broadcast_select_fusion
  25.8 7.3 all-to-all-start.1
  33.2 6.3 gather_fusion
  41.0 191.1 %all-reduce = f32[64]{0:T(128)S(1)} all-reduce(f32[64]{0:T(128)S(1)} %dynamic-update-slice), channel_id=1, replica_groups=mesh['image'=2,'orb'=16] {'orb'}, use_global_device_ids=true, to_apply=%add | all-reduce | flops 64 | bytes 512
  232.8 9.8 fusion.19
  242.6 9.7 gather_fusion.2
  252.4 9.8 fusion.22
  262.2 13.3 %broadcast_multiply_fusion = f32[48,200,200]{2,1,0:T(8,128)} fusion(bf16[48,512,200]{1,2,0:T(8,128)(2,1)} %fusion.19, bf16[48,512,200]{1,2,0:T(8,128)(2,1)} %fusion.22), kind=kOutput, calls=%fused_computation.39 | convolution fusion | flops 1968000000 | bytes 27340800 | tf_op jit(solution)/shard_map/pax,pbx->pab/dot_general | solution.py:44
  275.5 11.6 %copy.22 = f32[48,200,200]{1,2,0:T(8,128)} copy(f32[48,200,200]{2,1,0:T(8,128)} %broadcast_multiply_fusion) | data formatting | bytes 15360000 | tf_op jit(solution)/shard_map/mul | solution.py:44
  287.1 8.9 multiply_reduce_fusion
  296.2 22.3 %psum.14 = f32[64]{0:T(128)S(1)} all-reduce(f32[64]{0:T(128)S(1)} %add.167), channel_id=1, replica_groups=mesh['image'=2,'orb'=16] {'orb'}, use_global_device_ids=true, to_apply=%region_6.7 | all-reduce | flops 64 | bytes 512 | tf_op jit(solution)/shard_map/psum | solution.py:62
  318.7 11.3 %fusion.18 = f32[48]{0:T(128)S(1)} fusion(f32[48,200,200]{2,1,0:T(8,128)} %broadcast_multiply_fusion, f32[48,200,200]{1,2,0:T(8,128)} %copy.22, f32[48]{0:T(128)S(1)} %add.168, f32[48]{0:T(128)S(1)} %add.166, f32[48,200]{1,0:T(8,128)S(1)} %copy-done.3), kind=kLoop, calls=%fused_computation.31 | loop fusion | flops 36479952 | bytes 15398976 | tf_op jit(solution)/shard_map/reduce_sum | solution.py:56
  330.1 22.5 %psum.15 = f32[64]{0:T(128)S(1)} all-reduce(f32[64]{0:T(128)S(1)} %add.173), channel_id=1, replica_groups=mesh['image'=2,'orb'=16] {'orb'}, use_global_device_ids=true, to_apply=%region_12.13 | all-reduce | flops 64 | bytes 512 | tf_op jit(solution)/shard_map/psum | solution.py:62
  352.8 10.9 %divide_subtract_fusion = f32[48,200,200]{2,1,0:T(8,128)} fusion(f32[48,200,200]{2,1,0:T(8,128)} %broadcast_multiply_fusion, f32[48]{0:T(128)S(1)} %add.174, f32[48]{0:T(128)S(1)} %add.168, f32[48]{0:T(128)S(1)} %add.166, f32[48,200]{1,0:T(8,128)S(1)} %copy-done.3), kind=kLoop, calls=%fused_computation.26 | loop fusion | flops 26880000 | bytes 15398976 | tf_op jit(solution)/shard_map/sub | solution.py:67
  363.8 16.3 %convert_bitcast_fusion = bf16[48,256,512]{1,2,0:T(8,128)(2,1)} fusion(bf16[48,200,256]{2,1,0:T(8,128)(2,1)} %param.8, bf16[48,512,200]{1,2,0:T(8,128)(2,1)} %fusion.19, f32[48,200,200]{2,1,0:T(8,128)} %divide_subtract_fusion), kind=kOutput, calls=%fused_computation.7 | convolution fusion | flops 4495789056 | bytes 35008512 | tf_op jit(solution)/shard_map/pav,pax->pvx/dot_general | solution.py:78
  380.1 16.6 %copy.25 = bf16[48,256,512]{2,1,0:T(8,128)(2,1)} copy(bf16[48,256,512]{1,2,0:T(8,128)(2,1)} %convert_bitcast_fusion) | data formatting | bytes 25165824 | tf_op jit(solution)/shard_map/convert_element_type | solution.py:80
  396.7 14.7 %gather_fusion.3 = bf16[96,256,512]{2,1,0:T(8,128)(2,1)} fusion(bf16[48,256,512]{2,1,0:T(8,128)(2,1)} %copy.25, s32[1024]{0:T(1024)S(1)} %pad_clamp_fusion), kind=kCustom, calls=%fused_computation.3 | custom fusion | bytes 50332032 | tf_op jit(solution)/shard_map/jit(_take)/gather | solution.py:90
  411.4 21.3 %select_select_fusion = bf16[96,256,512]{2,1,0:T(8,128)(2,1)} fusion(bf16[96,256,512]{2,1,0:T(8,128)(2,1)} %gather_fusion.3, pred[96]{0:T(512)(128)(4,1)S(1)} %compare_and_fusion, pred[96]{0:T(512)(128)(4,1)S(1)} %fusion.39), kind=kLoop, calls=%fused_computation.6 | loop fusion | flops 25165824 | bytes 50331840 | tf_op jit(solution)/shard_map/jit(_where)/select_n | solution.py:90
  432.7 17.3 %all-to-all-start.2 = ((bf16[96,256,512]{2,1,0:T(8,128)(2,1)}), bf16[96,256,512]{2,1,0:T(8,128)(2,1)}, u32[]{:S(2)}, u32[]{:S(2)}) async-start(bf16[96,256,512]{2,1,0:T(8,128)(2,1)} %select_select_fusion), calls=%async_computation.2 | async-start | bytes 50331648 | tf_op jit(solution)/shard_map/all_to_all | solution.py:91
  450.2 16.1 %convert_bitcast_fusion.1 = bf16[48,256,512]{1,2,0:T(8,128)(2,1)} fusion(bf16[48,200,256]{2,1,0:T(8,128)(2,1)} %param.8, bf16[48,512,200]{1,2,0:T(8,128)(2,1)} %fusion.22, f32[48,200,200]{2,1,0:T(8,128)} %divide_subtract_fusion), kind=kOutput, calls=%fused_computation.8 | convolution fusion | flops 4495789056 | bytes 35008512 | tf_op jit(solution)/shard_map/pav,pax->pvx/dot_general | solution.py:75
  466.3 17.4 %copy.23 = bf16[48,256,512]{2,0,1:T(8,128)(2,1)} copy(bf16[48,256,512]{1,2,0:T(8,128)(2,1)} %convert_bitcast_fusion.1) | data formatting | bytes 25165824 | tf_op jit(solution)/shard_map/convert_element_type | solution.py:77
  483.7 508.2 %all-to-all-done.2 = bf16[96,256,512]{2,1,0:T(8,128)(2,1)} async-done(((bf16[96,256,512]{2,1,0:T(8,128)(2,1)}), bf16[96,256,512]{2,1,0:T(8,128)(2,1)}, u32[]{:S(2)}, u32[]{:S(2)}) %all-to-all-start.2) | async-done | bytes 25165856 | tf_op jit(solution)/shard_map/all_to_all | solution.py:91
  991.9 25.3 %fusion = f32[4,256,512]{2,0,1:T(4,128)} fusion(bf16[96,256,512]{2,1,0:T(8,128)(2,1)} %all-to-all-done.2, s32[96]{0:T(128)S(1)} %eq.108), kind=kOutput, calls=%fused_computation.4 | convolution fusion | flops 100663680 | bytes 27263360 | tf_op jit(solution)/shard_map/or,rvx->ovx/dot_general | solution.py:94
  (70 shorter events, 14.7 us)
Async XLA Ops:
  0.6 12.4 %copy-start = (bf16[4,256,512]{2,1,0:T(8,128)(2,1)S(1)}, bf16[4,256,512]{2,1,0:T(8,128)(2,1)}, u32[]{:S(2)}) copy-start(bf16[4,256,512]{2,1,0:T(8,128)(2,1)} %param.7) | copy-start | bytes 3145732
  12.9 12.9 %copy-start.6 = (s32[32]{0:T(128)}, s32[32]{0:T(128)S(1)}, u32[]{:S(2)}) copy-start(s32[32]{0:T(128)S(1)} %all_to_all.18) | copy-start | bytes 388
  25.8 7.3 copy-start.4
  25.8 216.8 %all-to-all-start.1 = ((bf16[32,256,512]{2,1,0:T(8,128)(2,1)}), bf16[32,256,512]{2,1,0:T(8,128)(2,1)}, u32[]{:S(2)}, u32[]{:S(2)}) async-start(bf16[32,256,512]{2,1,0:T(8,128)(2,1)} %broadcast_select_fusion), calls=%async_computation.1 | async-start | bytes 16777216 | tf_op jit(solution)/shard_map/all_to_all | solution.py:27
  33.2 6.3 copy-start.11
  33.2 7.5 copy-start.9
  33.2 198.9 %copy-start.8 = (s32[32]{0:T(128)S(1)}, s32[32]{0:T(128)}, u32[]{:S(2)}) copy-start(s32[32]{0:T(128)} %param.12) | copy-start | bytes 388
  33.2 198.9 %copy-start.10 = (s32[48,1]{0,1:T(1,128)S(1)}, s32[48,1]{0,1:T(1,128)}, u32[]{:S(2)}) copy-start(s32[48,1]{0,1:T(1,128)} %param.13) | copy-start | bytes 580
  275.5 11.6 %copy-start.3 = (f32[48,200]{1,0:T(8,128)S(1)}, f32[48,200]{1,0:T(8,128)}, u32[]{:S(2)}) copy-start(f32[48,200]{1,0:T(8,128)} %param.9) | copy-start | bytes 115204
  432.7 17.3 %copy-start.7 = (s32[32]{0:T(128)S(1)}, s32[32]{0:T(128)}, u32[]{:S(2)}) copy-start(s32[32]{0:T(128)} %copy-done.6) | copy-start | bytes 388
  432.7 559.2 %all-to-all-start.2 = ((bf16[96,256,512]{2,1,0:T(8,128)(2,1)}), bf16[96,256,512]{2,1,0:T(8,128)(2,1)}, u32[]{:S(2)}, u32[]{:S(2)}) async-start(bf16[96,256,512]{2,1,0:T(8,128)(2,1)} %select_select_fusion), calls=%async_computation.2 | async-start | bytes 50331648 | tf_op jit(solution)/shard_map/all_to_all | solution.py:91
  483.7 533.5 %copy-start.5 = (s32[48]{0:T(128)S(1)}, s32[48]{0:T(128)}, u32[]{:S(2)}) copy-start(s32[48]{0:T(128)} %param.11) | copy-start | bytes 580
  991.9 25.4 %copy-start.2 = (bf16[48,256,512]{2,0,1:T(8,128)(2,1)S(1)}, bf16[48,256,512]{2,0,1:T(8,128)(2,1)}, u32[]{:S(2)}) copy-start(bf16[48,256,512]{2,0,1:T(8,128)(2,1)} %copy.23) | copy-start | bytes 37748740
  991.9 30.4 %copy-start.1 = (bf16[4,256,512]{2,1,0:T(8,128)(2,1)S(1)}, bf16[4,256,512]{2,1,0:T(8,128)(2,1)}, u32[]{:S(2)}) copy-start(bf16[4,256,512]{2,1,0:T(8,128)(2,1)} %param.7) | copy-start | bytes 3145732
where the time goes:
time: 1020 us
  waiting for transfers between devices  508 us (50%)
  blocking collectives  246 us (24%)
  matrix products  93.8 us (9%)
  local copies, waits for them, and re-layouts  86 us (8%)
  other arithmetic  62.1 us (6%)
  starting transfers between devices  24.6 us (2%)
    all_to_all x1, waiting for transfers between devices, on_device(): lax.all_to_all(sending, 'orb', split_axis=0, concat_axis=0, tiled=True)  508 us
    unnamed x1, blocking collectives  191 us
    psum x2, blocking collectives, on_device(): shifts = shift_weight * lax.psum(partial_energy, 'orb')  44.8 us
    dot_general x1, matrix products, on_device(): jnp.einsum('or,rvx->ovx', home_hot, home_terms, preferred_element_type=jn...  25.3 us
    select_n x1, other arithmetic, on_device(): jnp.where(filled[:, None, None], jnp.take(second_pao, row_pair, axis=0),...  21.3 us
  transfers between devices with their start and end apart: 2, of which 1 were waited for; matrix products, arithmetic and copies ran while one was open for 5% of the time, Pallas kernels for 0%

commit v1 on v0

v1 whole, which is shorter than its diff:
```python
import functools

import jax
import jax.numpy as jnp
from jax import lax
from jax.experimental import pallas as pl
from jax.experimental.pallas import tpu as pltpu
from jax.sharding import PartitionSpec as P

ITERS = 2
shift_weight = 0.1
MESH = pl.DeviceIdType.MESH
F32 = jnp.float32
BF16 = jnp.bfloat16
VMEM_LIMIT = 56 * 1024 * 1024


def chip_at(position, chips):
    position = lax.rem(position + 2 * chips, chips)
    if chips == 8:
        far = position // 4
        return 2 * (position + far * (7 - 2 * position)) + far
    return position


def place_of(chip, chips):
    if chips == 8:
        y = lax.rem(chip, 2)
        z = chip // 2
        return z + y * (7 - 2 * z)
    return chip


def ring(n):
    me = lax.axis_index("orb")
    chips = n // 2
    core = lax.rem(me, 2)
    place = place_of(me // 2, chips)

    def dev(position, c):
        return chip_at(position, chips) * 2 + c

    return me, chips, core, place, dev


def greet(others):
    barrier = pltpu.get_barrier_semaphore()
    for other in others:
        pl.semaphore_signal(barrier, inc=1, device_id={"orb": other}, device_id_type=MESH)
    pl.semaphore_wait(barrier, len(others))


def remote(src, dst, send, recv, target):
    return pltpu.make_async_remote_copy(
        src_ref=src, dst_ref=dst, send_sem=send, recv_sem=recv, device_id={"orb": target}, device_id_type=MESH
    )


def gather_kernel(n, x_ref, info_ref, out_ref, info_out, ring_send, ring_recv, sib_send, sib_recv, info_send, info_recv, own_sem):
    me, chips, core, place, dev = ring(n)
    orbs = x_ref.shape[0]
    half = orbs // 2
    greet([lax.rem(me + d, n) for d in range(1, n)])
    ends = (dev(place + 1, core), dev(place - 1, core))
    sibling = me + 1 - 2 * core
    waits = []

    def row(position, way, k):
        return dev(position, core) * orbs + way * half + k

    arrivals = []
    for step in range(chips):
        incoming = []
        for k in range(half):
            for way in range(2):
                position = place - step if way == 0 else place + step
                r = row(position, way, k)
                if step == 0:
                    src = x_ref.at[way * half + k]
                else:
                    arrivals[step - 1][k * 2 + way].wait_recv()
                    src = out_ref.at[r]
                if step < chips - 1:
                    copy = remote(src, out_ref.at[r], ring_send.at[way, step, k], ring_recv.at[way, step, k], ends[way])
                    copy.start()
                    incoming.append(copy)
                    waits.append(copy.wait_send)
                side = remote(src, out_ref.at[r], sib_send.at[way, step, k], sib_recv.at[way, step, k], sibling)
                side.start()
                waits.append(side.wait_send)
                waits.append(side.wait_recv)
        arrivals.append(incoming)
        if step == 0:
            own = pltpu.make_async_copy(x_ref, out_ref.at[pl.ds(me * orbs, orbs)], own_sem.at[0])
            own.start()
            waits.append(own.wait)
            for d in range(1, n):
                note = remote(info_ref, info_out.at[me], info_send.at[d - 1], info_recv.at[d - 1], lax.rem(me + d, n))
                note.start()
                waits.append(note.wait_send)
                waits.append(note.wait_recv)
            info_out[me] = info_ref[...]
    for wait in waits:
        wait()


def gather(n, x, info):
    chips, half = n // 2, x.shape[0] // 2
    dma = pltpu.SemaphoreType.DMA
    return pl.pallas_call(
        functools.partial(gather_kernel, n),
        name="gather_blocks",
        out_shape=(
            jax.ShapeDtypeStruct((n * x.shape[0],) + x.shape[1:], x.dtype),
            jax.ShapeDtypeStruct((n,) + info.shape, info.dtype),
        ),
        in_specs=[pl.BlockSpec(memory_space=pl.ANY), pl.BlockSpec(memory_space=pltpu.VMEM)],
        out_specs=(pl.BlockSpec(memory_space=pl.ANY), pl.BlockSpec(memory_space=pltpu.VMEM)),
        scratch_shapes=[
            dma((2, chips, half)), dma((2, chips, half)), dma((2, chips, half)), dma((2, chips, half)),
            dma((n - 1,)), dma((n - 1,)), dma((1,)),
        ],
        compiler_params=pltpu.CompilerParams(collective_id=0, has_side_effects=True, vmem_limit_bytes=VMEM_LIMIT),
    )(x, info)


def coulomb_kernel(group, orbs, first_s, second_s, fglob_s, info_s, x_ref, pno_ref, level_ref, *rest):
    blocks = rest[:group]
    fp_ref, sp_ref, c_ref, e_ref = rest[group:]
    step = pl.program_id(0)
    width = pno_ref.shape[1]
    scale = x_ref.shape[2] ** -0.5
    lane = lax.broadcasted_iota(jnp.int32, (1, 128), 1)

    @pl.when(step == 0)
    def _():
        e_ref[...] = jnp.zeros_like(e_ref)
        e_ref[2:4, :] = jnp.full((2, 128), -1.0, F32)

    for j in range(group):
        p = step * group + j
        fg, sg = fglob_s[p], second_s[p]
        w = pno_ref[j]
        fp = jnp.dot(w, x_ref[first_s[p]], preferred_element_type=F32).astype(BF16)
        sp = jnp.dot(w, blocks[j][0], preferred_element_type=F32).astype(BF16)
        c = lax.dot_general(fp, sp, (((1,), (1,)), ((), ())), preferred_element_type=F32) * scale
        levels = jnp.broadcast_to(level_ref[0, j:j + 1, :], (width, width))
        occ = info_s[fg // orbs, lax.rem(fg, orbs)] + info_s[sg // orbs, lax.rem(sg, orbs)]
        inverse = 1.0 / (levels + levels.T - occ)
        t = c * (2.0 * c - c.T) * inverse
        norm = -1.0 / (width * width)
        e0 = jnp.sum(t) * norm
        e1 = jnp.sum(t * inverse) * norm
        fp_ref[j] = fp
        sp_ref[j] = sp
        c_ref[j] = c
        here = lane == p
        e_ref[0:1, :] = jnp.where(here, e0, e_ref[0:1, :])
        e_ref[1:2, :] = jnp.where(here, e1, e_ref[1:2, :])
        e_ref[2:3, :] = jnp.where(here, fg.astype(F32), e_ref[2:3, :])
        e_ref[3:4, :] = jnp.where(here, sg.astype(F32), e_ref[3:4, :])


def group_of(pairs):
    return next(g for g in (4, 3, 2, 1) if pairs % g == 0)


def coulomb_call(first_local, second, first_glob, info, x, gathered, pno, levels):
    pairs, width, nvirt = pno.shape
    aux = x.shape[2]
    group = group_of(pairs)

    def second_map(j, i, fl, sg, fg):
        return (sg[i * group + j], 0, 0)

    three = lambda i, *_: (i, 0, 0)
    zero3 = lambda i, *_: (0, 0, 0)
    return pl.pallas_call(
        functools.partial(coulomb_kernel, group, x.shape[0]),
        name="coulomb",
        out_shape=(
            jax.ShapeDtypeStruct((pairs, width, aux), BF16),
            jax.ShapeDtypeStruct((pairs, width, aux), BF16),
            jax.ShapeDtypeStruct((pairs, width, width), F32),
            jax.ShapeDtypeStruct((8, 128), F32),
        ),
        grid_spec=pltpu.PrefetchScalarGridSpec(
            num_scalar_prefetch=3,
            grid=(pairs // group,),
            in_specs=[
                pl.BlockSpec(memory_space=pltpu.SMEM),
                pl.BlockSpec(x.shape, zero3),
                pl.BlockSpec((group, width, nvirt), three),
                pl.BlockSpec((1, group, width), three),
            ] + [pl.BlockSpec((1, nvirt, aux), functools.partial(second_map, j)) for j in range(group)],
            out_specs=(
                pl.BlockSpec((group, width, aux), three),
                pl.BlockSpec((group, width, aux), three),
                pl.BlockSpec((group, width, width), three),
                pl.BlockSpec((8, 128), lambda i, *_: (0, 0)),
            ),
        ),
        compiler_params=pltpu.CompilerParams(vmem_limit_bytes=VMEM_LIMIT),
    )(first_local, second, first_glob, info, x, pno, levels.reshape(pairs // group, group, width), *([gathered] * group))


def shift_kernel(n, orb_total, e_ref, out_ref, got, send, recv):
    me = lax.axis_index("orb")
    greet([lax.rem(me + d, n) for d in range(1, n)])
    copies = []
    for d in range(1, n):
        copy = remote(e_ref, got.at[me], send.at[d - 1], recv.at[d - 1], lax.rem(me + d, n))
        copy.start()
        copies.append(copy)
    got[me] = e_ref[...]
    for copy in copies:
        copy.wait()
    ids = lax.broadcasted_iota(jnp.int32, (orb_total, 128), 0).astype(F32)

    def shares(block):
        return jnp.where(ids == block[2:3, :], 1.0, 0.0) + jnp.where(ids == block[3:4, :], 1.0, 0.0)

    total = jnp.zeros((orb_total, 128), F32)
    for d in range(n):
        block = got[d]
        total = total + shares(block) * block[0:1, :]
    shift = shift_weight * jnp.sum(total, axis=1, keepdims=True)
    total = jnp.zeros((orb_total, 128), F32)
    for d in range(n):
        block = got[d]
        hot = shares(block)
        pair_shift = jnp.sum(hot * shift, axis=0, keepdims=True)
        total = total + hot * (block[0:1, :] - pair_shift * block[1:2, :])
    shift2 = shift_weight * jnp.sum(total, axis=1, keepdims=True)
    mine = shares(e_ref[...])
    out_ref[...] = jnp.zeros_like(out_ref)
    out_ref[0:1, :] = jnp.sum(mine * shift, axis=0, keepdims=True)
    out_ref[1:2, :] = jnp.sum(mine * shift2, axis=0, keepdims=True)


def shift_call(n, orb_total, energies):
    dma = pltpu.SemaphoreType.DMA
    return pl.pallas_call(
        functools.partial(shift_kernel, n, orb_total),
        name="shifts",
        out_shape=jax.ShapeDtypeStruct((8, 128), F32),
        in_specs=[pl.BlockSpec(memory_space=pltpu.VMEM)],
        out_specs=pl.BlockSpec(memory_space=pltpu.VMEM),
        scratch_shapes=[pltpu.VMEM((n, 8, 128), F32), dma((n - 1,)), dma((n - 1,))],
        compiler_params=pltpu.CompilerParams(collective_id=1, has_side_effects=True, vmem_limit_bytes=VMEM_LIMIT),
    )(energies)


def density_kernel(group, orbs, first_s, slot_s, second_s, fglob_s, fresh_s, final_s, seen_s,
                   info_s, shift_s, pno_ref, level_ref, fp_ref, sp_ref, c_ref,
                   amp_ref, dens_ref, terms_ref, acc, stage, blank, busy, stage_sem, blank_sem):
    step = pl.program_id(0)
    width = pno_ref.shape[1]
    aux = fp_ref.shape[2]
    total = terms_ref.shape[0]

    def blank_copy(o):
        return pltpu.make_async_copy(blank, terms_ref.at[o], blank_sem.at[0])

    @pl.when(step == 0)
    def _():
        dens_ref[...] = jnp.zeros_like(dens_ref)
        blank[...] = jnp.zeros_like(blank)
        for j in range(group):
            busy[j] = 0

        @pl.loop(0, total)
        def _(o):
            @pl.when(seen_s[o] == 0)
            def _():
                blank_copy(o).start()

    for j in range(group):
        p = step * group + j
        fg, sg, slot = fglob_s[p], second_s[p], slot_s[p]
        levels = jnp.broadcast_to(level_ref[0, j:j + 1, :], (width, width))
        occ = info_s[fg // orbs, lax.rem(fg, orbs)] + info_s[sg // orbs, lax.rem(sg, orbs)]
        inverse = 1.0 / (levels + levels.T - occ)
        s1, s2 = shift_s[0, p], shift_s[1, p]
        amp = -c_ref[j] * inverse * (1.0 - s2 * inverse * (1.0 - s1 * inverse))
        amp_ref[j] = amp
        half = amp.astype(BF16)
        part1 = jnp.dot(half, sp_ref[j], preferred_element_type=F32).astype(BF16)
        part2 = lax.dot_general(half, fp_ref[j], (((0,), (0,)), ((), ())), preferred_element_type=F32).astype(BF16)
        parts = jnp.concatenate([part1, part2], axis=1)
        pao = lax.dot_general(pno_ref[j], parts, (((0,), (0,)), ((), ())), preferred_element_type=F32)
        dens_ref[first_s[p]] += pao[:, :aux]
        term = pao[:, aux:]
        acc[slot] = jnp.where(fresh_s[p] == 1, term, acc[slot] + term)

        @pl.when(final_s[p] == 1)
        def _():
            copy = pltpu.make_async_copy(stage.at[j], terms_ref.at[sg], stage_sem.at[j])

            @pl.when(busy[j] == 1)
            def _():
                copy.wait()

            stage[j] = acc[slot].astype(BF16)
            copy.start()
            busy[j] = 1

    @pl.when(step == pl.num_programs(0) - 1)
    def _():
        for j in range(group):
            @pl.when(busy[j] == 1)
            def _():
                pltpu.make_async_copy(stage.at[j], terms_ref.at[0], stage_sem.at[j]).wait()

        @pl.loop(0, total)
        def _(o):
            @pl.when(seen_s[o] == 0)
            def _():
                blank_copy(o).wait()


def density_call(scalars, info, shifts, orbs, slots, orb_total, pno, levels, fp, sp, c):
    pairs, width, nvirt = pno.shape
    aux = fp.shape[2]
    group = group_of(pairs)
    three = lambda i, *_: (i, 0, 0)
    smem = pl.BlockSpec(memory_space=pltpu.SMEM)
    dma = pltpu.SemaphoreType.DMA
    return pl.pallas_call(
        functools.partial(density_kernel, group, orbs),
        name="density_terms",
        out_shape=(
            jax.ShapeDtypeStruct((pairs, width, width), F32),
            jax.ShapeDtypeStruct((orbs, nvirt, aux), F32),
            jax.ShapeDtypeStruct((orb_total, nvirt, aux), BF16),
        ),
        grid_spec=pltpu.PrefetchScalarGridSpec(
            num_scalar_prefetch=7,
            grid=(pairs // group,),
            in_specs=[
                smem, smem,
                pl.BlockSpec((group, width, nvirt), three),
                pl.BlockSpec((1, group, width), three),
                pl.BlockSpec((group, width, aux), three),
                pl.BlockSpec((group, width, aux), three),
                pl.BlockSpec((group, width, width), three),
            ],
            out_specs=(
                pl.BlockSpec((group, width, width), three),
                pl.BlockSpec((orbs, nvirt, aux), lambda i, *_: (0, 0, 0)),
                pl.BlockSpec(memory_space=pl.ANY),
            ),
            scratch_shapes=[
                pltpu.VMEM((slots, nvirt, aux), F32),
                pltpu.VMEM((group, nvirt, aux), BF16),
                pltpu.VMEM((nvirt, aux), BF16),
                pltpu.SMEM((group,), jnp.int32),
                dma((group,)), dma((1,)),
            ],
        ),
        compiler_params=pltpu.CompilerParams(vmem_limit_bytes=VMEM_LIMIT),
    )(*scalars, info, shifts, pno, levels.reshape(pairs // group, group, width), fp, sp, c)


def home_kernel(n, terms_ref, dens_ref, out_ref, own, side, got, own_sem, side_send, side_recv, ring_send, ring_recv):
    me, chips, core, place, dev = ring(n)
    orbs, rows = dens_ref.shape[0], dens_ref.shape[1]
    half = orbs // 2
    sibling = me + 1 - 2 * core
    ends = (dev(place + 1, core), dev(place - 1, core))
    greet([ends[0], ends[1], sibling])
    chunk = 32

    def position(way, step):
        return place - 1 - step if way == 0 else place + 1 + step

    def own_copy(way, step, k):
        r = dev(position(way, step), core) * orbs + way * half + k
        return pltpu.make_async_copy(terms_ref.at[r], own.at[way, step, k], own_sem.at[way, step, k])

    def side_copy(way, step, k):
        r = dev(position(way, step), 1 - core) * orbs + way * half + k
        return remote(terms_ref.at[r], side.at[way, step, k], side_send.at[way, step, k], side_recv.at[way, step, k], sibling)

    def load(step):
        for k in range(half):
            for way in range(2):
                side_copy(way, step, k).start()
                own_copy(way, step, k).start()

    def ring_copy(way, step, k):
        return remote(side.at[way, step, k], got.at[way, step, k], ring_send.at[way, step, k], ring_recv.at[way, step, k], ends[way])

    load(0)
    load(1)
    for step in range(chips):
        for k in range(half):
            for way in range(2):
                own_copy(way, step, k).wait()
                side_copy(way, step, k).wait_recv()
                if step > 0:
                    ring_copy(way, step - 1, k).wait_recv()

                @pl.loop(0, rows // chunk)
                def _(i):
                    at = pl.ds(pl.multiple_of(i * chunk, chunk), chunk)
                    total = own[way, step, k, at, :].astype(F32) + side[way, step, k, at, :].astype(F32)
                    if step > 0:
                        total = total + got[way, step - 1, k, at, :].astype(F32)
                    if step < chips - 1:
                        side[way, step, k, at, :] = total.astype(BF16)
                    else:
                        out_ref[way * half + k, at, :] = dens_ref[way * half + k, at, :] + total

                if step < chips - 1:
                    ring_copy(way, step, k).start()
        if step + 2 < chips:
            load(step + 2)
    for step in range(chips):
        for k in range(half):
            for way in range(2):
                side_copy(way, step, k).wait_send()
                if step < chips - 1:
                    ring_copy(way, step, k).wait_send()


def home(n, terms, density):
    orbs, nvirt, aux = density.shape
    chips, half = n // 2, orbs // 2
    dma = pltpu.SemaphoreType.DMA
    many = (2, chips, half)
    return pl.pallas_call(
        functools.partial(home_kernel, n),
        name="terms_home",
        out_shape=jax.ShapeDtypeStruct(density.shape, F32),
        in_specs=[pl.BlockSpec(memory_space=pl.ANY), pl.BlockSpec(memory_space=pltpu.VMEM)],
        out_specs=pl.BlockSpec(memory_space=pltpu.VMEM),
        scratch_shapes=[
            pltpu.VMEM(many + (nvirt, aux), BF16),
            pltpu.VMEM(many + (nvirt, aux), BF16),
            pltpu.VMEM((2, chips - 1, half, nvirt, aux), BF16),
            dma(many), dma(many), dma(many), dma(many), dma(many),
        ],
        compiler_params=pltpu.CompilerParams(collective_id=2, has_side_effects=True, vmem_limit_bytes=VMEM_LIMIT),
    )(terms, density)


def on_device(orb_blocks, pno, pno_levels, occ_levels, pair_i_local, fetch_local, pair_slot):
    n = lax.axis_size("orb")
    orbs = orb_blocks.shape[0]
    pairs = pno.shape[0]
    slots = fetch_local.shape[0]
    orb_total = orbs * n
    per_owner = slots // n
    slot_of = pair_slot[:, 0]
    slot_ids = jnp.arange(slots, dtype=jnp.int32)
    pair_ids = jnp.arange(pairs, dtype=jnp.int32)
    slot_orb = slot_ids // per_owner * orbs + fetch_local
    first_glob = lax.axis_index("orb") * orbs + pair_i_local
    second = jnp.sum(jnp.where(slot_of[:, None] == slot_ids[None, :], slot_orb[None, :], 0), axis=1)
    same = slot_of[:, None] == slot_of[None, :]
    fresh = 1 - jnp.any(same & (pair_ids[None, :] < pair_ids[:, None]), axis=1).astype(jnp.int32)
    final = 1 - jnp.any(same & (pair_ids[None, :] > pair_ids[:, None]), axis=1).astype(jnp.int32)
    seen = jnp.any(second[:, None] == jnp.arange(orb_total, dtype=jnp.int32)[None, :], axis=0).astype(jnp.int32)
    info = jnp.pad(occ_levels[None, :], ((0, 7), (0, 128 - orbs)))
    gathered, info_all = gather(n, orb_blocks, info)
    info_all = info_all[:, 0, :orbs]
    fp, sp, coulomb, energies = coulomb_call(
        pair_i_local, second, first_glob, info_all, orb_blocks, gathered, pno, pno_levels
    )
    shifts = shift_call(n, orb_total, energies)
    scalars = (pair_i_local, slot_of, second, first_glob, fresh, final, seen)
    amplitude, density, terms = density_call(
        scalars, info_all, shifts, orbs, slots, orb_total, pno, pno_levels, fp, sp, coulomb
    )
    return (amplitude, home(n, terms, density))


def solution(mesh):
    placed = (
        P(("image", "orb"), None, None),
        P(("image", "orb"), None, None),
        P(("image", "orb"), None),
        P(("image", "orb")),
        P(("image", "orb")),
        P(("image", "orb")),
        P(("image", "orb"), None),
    )
    return jax.shard_map(
        on_device,
        mesh=mesh,
        in_specs=placed,
        out_specs=(P(("image", "orb"), None, None), P(("image", "orb"), None, None)),
        check_vma=False,
    )
```

time: 1020 us -> 266 us (0.26)
  waiting for transfers between devices: 508 us -> 0 us
  Pallas kernels: 0 us -> 251 us
  blocking collectives: 246 us -> 0 us
  matrix products: 93.8 us -> 0 us
  local copies, waits for them, and re-layouts: 86 us -> 7.2 us
  other arithmetic: 62.1 us -> 4.73 us
  starting transfers between devices: 24.6 us -> 0 us
    all_to_all x2 -> x0, waiting for transfers between devices: 508 us -> none  [the longest x1 508 us: on_device(): lax.all_to_all(sending, 'orb', split_axis=0, concat_axis=0, tiled=True)]
    pallas_call x0 -> x5, Pallas kernels: none -> 251 us  [the longest x1 89.8 us: gather(): pl.pallas_call(functools.partial(gather_kernel, n), name='gather_blocks',...]
    unnamed x1 -> x0, blocking collectives: 191 us -> none
    dot_general x7 -> x0, matrix products: 93.8 us -> none  [the longest x1 25.3 us: on_device(): jnp.einsum('or,rvx->ovx', home_hot, home_terms, preferred_element_type=jn...]
    psum x2 -> x0, blocking collectives: 44.8 us -> none  [on_device(): shifts = shift_weight * lax.psum(partial_energy, 'orb')]
    gather x4 -> x0, local copies, waits for them, and re-layouts: 35.8 us -> none  [the longest x1 14.7 us: on_device(): jnp.take(second_pao, row_pair, axis=0)]
    convert_element_type x2 -> x0, local copies, waits for them, and re-layouts: 34 us -> none  [the longest x1 17.4 us: on_device(): first_pao = jnp.einsum('pav,pax->pvx', pno, first_part, preferred_element...]
    select_n x5 -> x0, other arithmetic: 29 us -> none  [the longest x1 21.3 us: on_device(): jnp.where(filled[:, None, None], jnp.take(second_pao, row_pair, axis=0),...]
  transfers between devices with their start and end apart: 2 -> 0, of which waited for: 1 -> 0; matrix products, arithmetic and copies ran while one was open for 5% -> 0% of each run, Pallas kernels for 0% -> 0%
where the time goes in v1:
time: 266 us; the launch traced here: 263 us
  Pallas kernels  251 us (94%)
  local copies, waits for them, and re-layouts  7.2 us (3%)
  other arithmetic  4.73 us (2%)
    pallas_call x1, Pallas kernels, gather(): pl.pallas_call(functools.partial(gather_kernel, n), name='gather_blocks',...  89.8 us
    pallas_call x1, Pallas kernels, home(): pl.pallas_call(functools.partial(home_kernel, n), name='terms_home', out_...  88.7 us
    pallas_call x1, Pallas kernels, density_call(): pl.pallas_call(functools.partial(density_kernel, group, orbs), name='dens...  37.8 us
    pallas_call x1, Pallas kernels, coulomb_call(): pl.pallas_call(functools.partial(coulomb_kernel, group, x.shape[0]), name...  26.3 us
    pallas_call x1, Pallas kernels, shift_call(): pl.pallas_call(functools.partial(shift_kernel, n, orb_total), name='shift...  7.9 us

profile of v1, /device:TPU:15, one launch (start us, length us, event | category | flops | bytes accessed | tf_op | source)
XLA Modules:
  0.0 263.1 jit_solution(17624479985956261728)
XLA Ops:
  0.6 1.2 broadcast_add_fusion.fglob_s
  1.8 0.7 fusion.4
  2.5 0.7 select_reduce_fusion.second_s
  3.2 0.0 copy-start
  3.2 0.1 fusion.2
  3.3 0.5 convert_element_type.13.seen_s
  3.8 0.9 fusion.1
  4.8 0.6 convert_subtract_fusion
  5.4 1.3 pad.4.info_ref
  6.6 1.4 reshape.11.level_ref
  8.1 89.8 %gather_blocks.1 = (bf16[64,256,512]{2,1,0:T(8,128)(2,1)}, f32[16,8,128]{2,1,0:T(8,128)}) custom-call(bf16[4,256,512]{2,1,0:T(8,128)(2,1)} %x_ref.3, f32[8,128]{1,0:T(8,128)} %pad.4.info_ref), custom_call_target="tpu_custom_call" | custom-call | tf_op jit(solution)/shard_map/gather_blocks/pallas_call | solution.py:110
  97.9 1.4 slice.3
  99.3 0.0 copy-done
  99.3 26.3 %coulomb.1 = (bf16[48,200,512]{2,1,0:T(8,128)(2,1)}, bf16[48,200,512]{2,1,0:T(8,128)(2,1)}, f32[48,200,200]{2,1,0:T(8,128)}, f32[8,128]{1,0:T(8,128)}) custom-call(s32[48]{0:T(128)} %first_s.3, s32[48]{0:T(128)} %copy-done, s32[48]{0:T(128)} %broadcast_add_fusion.fglob_s, f32[16,4]{1,0:T(8,128)} %bitcast.3, bf16[4,256,512]{2,1,0:T(8,128)(2,1)} %x_ref.3, ...), custom_call_target="tpu_custom_call" | custom-call | tf_op jit(solution)/shard_map/coulomb/pallas_call | solution.py:178
  125.6 7.9 %shifts.1.shift_s = f32[8,128]{1,0:T(8,128)} custom-call(f32[8,128]{1,0:T(8,128)} %get-tuple-element.13.e_ref), custom_call_target="tpu_custom_call" | custom-call | tf_op jit(solution)/shard_map/shifts/pallas_call | solution.py:243
  133.5 37.8 %density_terms.1 = (f32[48,200,200]{2,1,0:T(8,128)}, f32[4,256,512]{2,1,0:T(8,128)}, bf16[64,256,512]{2,1,0:T(8,128)(2,1)}) custom-call(s32[48]{0:T(128)} %first_s.3, s32[48]{0:T(128)} %bitcast.7, s32[48]{0:T(128)} %copy-done, s32[48]{0:T(128)} %broadcast_add_fusion.fglob_s, s32[48]{0:T(128)} %get-tuple-element.23.fresh_s, s32[48]{0:T(128)} %get-tuple-element.22.final_s, ...), custom_call_target="tpu_custom_call" | custom-call | tf_op jit(solution)/shard_map/density_terms/pallas_call | solution.py:329
  171.3 88.7 %terms_home.1 = f32[4,256,512]{2,1,0:T(8,128)} custom-call(bf16[64,256,512]{2,1,0:T(8,128)(2,1)} %get-tuple-element.18.terms_ref, f32[4,256,512]{2,1,0:T(8,128)} %get-tuple-element.19.dens_ref), custom_call_target="tpu_custom_call" | custom-call | tf_op jit(solution)/shard_map/terms_home/pallas_call | solution.py:432
  260.0 3.1 %copy.17 = f32[4,256,512]{2,1,0:T(8,128)} copy(f32[4,256,512]{2,1,0:T(8,128)} %terms_home.1) | data formatting | bytes 4194304
Async XLA Ops:
  3.2 96.1 %copy-start = (s32[48]{0:T(128)}, s32[48]{0:T(128)S(1)}, u32[]{:S(2)}) copy-start(s32[48]{0:T(128)S(1)} %select_reduce_fusion.second_s) | copy-start | bytes 580

commit v2 on v1

--- a/solution.py
+++ b/solution.py
@@ -7,6 +7,7 @@
 from jax.experimental.pallas import tpu as pltpu
 from jax.sharding import PartitionSpec as P
 
+MOST = 3
 ITERS = 2
 shift_weight = 0.1
 MESH = pl.DeviceIdType.MESH
@@ -56,152 +57,194 @@
     )
 
 
-def gather_kernel(n, x_ref, info_ref, out_ref, info_out, ring_send, ring_recv, sib_send, sib_recv, info_send, info_recv, own_sem):
+def gather_kernel(n, per_owner, first_s, fetch_s, row_s, x_ref, pno_ref, level_ref, info_ref,
+                  fp_out, sp_out, c_out, e_ref, info_out,
+                  blocks, current, fp_stage, sp_stage, c_stage,
+                  own_sem, first_send, first_recv, ring_send, ring_recv, side_send, side_recv, info_send, info_recv, out_sem):
     me, chips, core, place, dev = ring(n)
     orbs = x_ref.shape[0]
     half = orbs // 2
+    width = pno_ref.shape[1]
+    rows = per_owner * MOST
+    scale = x_ref.shape[2] ** -0.5
+    norm = -1.0 / (width * width)
+    sibling = me + 1 - 2 * core
+    ends = (dev(place + 1, core), dev(place - 1, core))
+    lane = lax.broadcasted_iota(jnp.int32, (1, 128), 1)
     greet([lax.rem(me + d, n) for d in range(1, n)])
-    ends = (dev(place + 1, core), dev(place - 1, core))
-    sibling = me + 1 - 2 * core
-    waits = []
-
-    def row(position, way, k):
-        return dev(position, core) * orbs + way * half + k
-
-    arrivals = []
-    for step in range(chips):
-        incoming = []
+
+    def owner_at(way, step):
+        return dev(place - step if way == 0 else place + step, way)
+
+    def first_copy(k):
+        local = lax.rem(half * (1 - core) + k, orbs)
+        return remote(x_ref.at[local], blocks.at[me, local], first_send.at[k], first_recv.at[k], sibling)
+
+    def ring_copy(way, step, k):
+        block = blocks.at[owner_at(way, step - 1), half * core + k]
+        return remote(block, block, ring_send.at[way, step, k], ring_recv.at[way, step, k], ends[way])
+
+    def ring_wait(way, step, k):
+        block = blocks.at[owner_at(way, step), half * core + k]
+        remote(block, block, ring_send.at[way, step, k], ring_recv.at[way, step, k], ends[way]).wait_recv()
+
+    def side_copy(way, step, k):
+        block = blocks.at[owner_at(way, step), half * core + k]
+        return remote(block, block, side_send.at[way, step, k], side_recv.at[way, step, k], sibling)
+
+    def side_wait(way, step, k):
+        block = blocks.at[owner_at(way, step), half * (1 - core) + k]
+        remote(block, block, side_send.at[way, step, k], side_recv.at[way, step, k], sibling).wait_recv()
+
+    def note(d):
+        return remote(info_ref, info_out.at[me], info_send.at[d - 1], info_recv.at[d - 1], lax.rem(me + d, n))
+
+    def out_copies(way, owner, i):
+        row = owner * rows + i
+        return [
+            pltpu.make_async_copy(stage.at[way, i], out.at[row], out_sem.at[way, kind, i])
+            for kind, (stage, out) in enumerate(((fp_stage, fp_out), (sp_stage, sp_out), (c_stage, c_out)))
+        ]
+
+    def work(way, step):
+        owner = owner_at(way, step)
+        for s in range(per_owner):
+            local = fetch_s[owner * per_owner + s]
+            block = blocks[owner, 0]
+            for other in range(1, orbs):
+                block = jnp.where(local == other, blocks[owner, other], block)
+            current[...] = block
+            occ2 = jnp.sum(jnp.where(lane == local, info_out[owner, 0:1, :], 0.0), axis=1, keepdims=True)
+            for m in range(MOST):
+                i = s * MOST + m
+                row = owner * rows + i
+                named = row_s[row]
+                q = jnp.maximum(named, 0)
+                first = first_s[q]
+                w = pno_ref[q]
+                fp = jnp.dot(w, x_ref[first], preferred_element_type=F32).astype(BF16)
+                sp = jnp.dot(w, current[...], preferred_element_type=F32).astype(BF16)
+                c = lax.dot_general(fp, sp, (((1,), (1,)), ((), ())), preferred_element_type=F32) * scale
+                levels = jnp.broadcast_to(level_ref[q], (width, width))
+                occ1 = jnp.sum(jnp.where(lane == first, info_ref[0:1, :], 0.0), axis=1, keepdims=True)
+                inverse = 1.0 / (levels + levels.T - (occ1 + occ2))
+                t = c * (2.0 * c - c.T) * inverse
+                e0 = jnp.sum(t) * norm
+                e1 = jnp.sum(t * inverse) * norm
+                fp_stage[way, i] = fp
+                sp_stage[way, i] = sp
+                c_stage[way, i] = c
+                for copy in out_copies(way, owner, i):
+                    copy.start()
+                here = lane == row
+                id1 = jnp.where(named >= 0, me * orbs + first, -1).astype(F32)
+                id2 = jnp.where(named >= 0, owner * orbs + local, -1).astype(F32)
+                e_ref[0:1, :] = jnp.where(here, e0, e_ref[0:1, :])
+                e_ref[1:2, :] = jnp.where(here, e1, e_ref[1:2, :])
+                e_ref[2:3, :] = jnp.where(here, id1, e_ref[2:3, :])
+                e_ref[3:4, :] = jnp.where(here, id2, e_ref[3:4, :])
+
+    for k in range(orbs):
+        first_copy(k).start()
+    own = pltpu.make_async_copy(x_ref, blocks.at[me], own_sem.at[0])
+    own.start()
+    own.wait()
+    for k in range(half):
+        first_copy(k).wait_recv()
+    for k in range(half):
+        for way in range(2):
+            ring_copy(way, 1, k).start()
+    for d in range(1, n):
+        note(d).start()
+    info_out[me] = info_ref[...]
+    e_ref[...] = jnp.zeros_like(e_ref)
+    e_ref[2:4, :] = jnp.full((2, 128), -1.0, F32)
+    for k in range(half, orbs):
+        first_copy(k).wait_recv()
+    for d in range(1, n):
+        note(d).wait()
+
+    def turn(step, carry):
+        for k in range(half):
+            @pl.when(step < chips)
+            def _():
+                for way in range(2):
+                    ring_wait(way, step, k)
+
+                    @pl.when(step < chips - 1)
+                    def _():
+                        ring_copy(way, step + 1, k).start()
+
+                    side_copy(way, step, k).start()
+
+            for way in range(2):
+                if way % half == k:
+                    @pl.when(step > 1)
+                    def _():
+                        for kk in range(half):
+                            side_wait(way, step - 1, kk)
+                        for i in range(rows):
+                            for copy in out_copies(way, owner_at(way, step - 2), i):
+                                copy.wait()
+
+                    work(way, step - 1)
+        return carry
+
+    lax.fori_loop(1, chips + 1, turn, 0)
+    for way in range(2):
+        for i in range(rows):
+            for copy in out_copies(way, owner_at(way, chips - 1), i):
+                copy.wait()
+    for k in range(orbs):
+        first_copy(k).wait_send()
+
+    def drain(step, carry):
         for k in range(half):
             for way in range(2):
-                position = place - step if way == 0 else place + step
-                r = row(position, way, k)
-                if step == 0:
-                    src = x_ref.at[way * half + k]
-                else:
-                    arrivals[step - 1][k * 2 + way].wait_recv()
-                    src = out_ref.at[r]
-                if step < chips - 1:
-                    copy = remote(src, out_ref.at[r], ring_send.at[way, step, k], ring_recv.at[way, step, k], ends[way])
-                    copy.start()
-                    incoming.append(copy)
-                    waits.append(copy.wait_send)
-                side = remote(src, out_ref.at[r], sib_send.at[way, step, k], sib_recv.at[way, step, k], sibling)
-                side.start()
-                waits.append(side.wait_send)
-                waits.append(side.wait_recv)
-        arrivals.append(incoming)
-        if step == 0:
-            own = pltpu.make_async_copy(x_ref, out_ref.at[pl.ds(me * orbs, orbs)], own_sem.at[0])
-            own.start()
-            waits.append(own.wait)
-            for d in range(1, n):
-                note = remote(info_ref, info_out.at[me], info_send.at[d - 1], info_recv.at[d - 1], lax.rem(me + d, n))
-                note.start()
-                waits.append(note.wait_send)
-                waits.append(note.wait_recv)
-            info_out[me] = info_ref[...]
-    for wait in waits:
-        wait()
-
-
-def gather(n, x, info):
-    chips, half = n // 2, x.shape[0] // 2
+                ring_copy(way, step, k).wait_send()
+                side_copy(way, step, k).wait_send()
+        return carry
+
+    lax.fori_loop(1, chips, drain, 0)
+
+
+def gather(n, first_local, fetch_local, row_pair, x, pno, levels, info):
+    pairs, width, nvirt = pno.shape
+    orbs, _, aux = x.shape
+    per_owner = fetch_local.shape[0] // n
+    rows = per_owner * MOST
+    total = rows * n
+    chips, half = n // 2, orbs // 2
     dma = pltpu.SemaphoreType.DMA
+    smem, vmem, anywhere = (pl.BlockSpec(memory_space=m) for m in (pltpu.SMEM, pltpu.VMEM, pl.ANY))
     return pl.pallas_call(
-        functools.partial(gather_kernel, n),
-        name="gather_blocks",
+        functools.partial(gather_kernel, n, per_owner),
+        name="gather_coulomb",
         out_shape=(
-            jax.ShapeDtypeStruct((n * x.shape[0],) + x.shape[1:], x.dtype),
+            jax.ShapeDtypeStruct((total, width, aux), BF16),
+            jax.ShapeDtypeStruct((total, width, aux), BF16),
+            jax.ShapeDtypeStruct((total, width, width), F32),
+            jax.ShapeDtypeStruct((8, 128), F32),
             jax.ShapeDtypeStruct((n,) + info.shape, info.dtype),
         ),
-        in_specs=[pl.BlockSpec(memory_space=pl.ANY), pl.BlockSpec(memory_space=pltpu.VMEM)],
-        out_specs=(pl.BlockSpec(memory_space=pl.ANY), pl.BlockSpec(memory_space=pltpu.VMEM)),
+        in_specs=[smem, smem, smem, vmem, vmem, vmem, vmem],
+        out_specs=(anywhere, anywhere, anywhere, vmem, vmem),
         scratch_shapes=[
+            pltpu.VMEM((n, orbs, nvirt, aux), BF16),
+            pltpu.VMEM((nvirt, aux), BF16),
+            pltpu.VMEM((2, rows, width, aux), BF16),
+            pltpu.VMEM((2, rows, width, aux), BF16),
+            pltpu.VMEM((2, rows, width, width), F32),
+            dma((1,)), dma((orbs,)), dma((orbs,)),
             dma((2, chips, half)), dma((2, chips, half)), dma((2, chips, half)), dma((2, chips, half)),
-            dma((n - 1,)), dma((n - 1,)), dma((1,)),
+            dma((n - 1,)), dma((n - 1,)), dma((2, 3, rows)),
         ],
         compiler_params=pltpu.CompilerParams(collective_id=0, has_side_effects=True, vmem_limit_bytes=VMEM_LIMIT),
-    )(x, info)
-
-
-def coulomb_kernel(group, orbs, first_s, second_s, fglob_s, info_s, x_ref, pno_ref, level_ref, *rest):
-    blocks = rest[:group]
-    fp_ref, sp_ref, c_ref, e_ref = rest[group:]
-    step = pl.program_id(0)
-    width = pno_ref.shape[1]
-    scale = x_ref.shape[2] ** -0.5
-    lane = lax.broadcasted_iota(jnp.int32, (1, 128), 1)
-
-    @pl.when(step == 0)
-    def _():
-        e_ref[...] = jnp.zeros_like(e_ref)
-        e_ref[2:4, :] = jnp.full((2, 128), -1.0, F32)
-
-    for j in range(group):
-        p = step * group + j
-        fg, sg = fglob_s[p], second_s[p]
-        w = pno_ref[j]
-        fp = jnp.dot(w, x_ref[first_s[p]], preferred_element_type=F32).astype(BF16)
-        sp = jnp.dot(w, blocks[j][0], preferred_element_type=F32).astype(BF16)
-        c = lax.dot_general(fp, sp, (((1,), (1,)), ((), ())), preferred_element_type=F32) * scale
-        levels = jnp.broadcast_to(level_ref[0, j:j + 1, :], (width, width))
-        occ = info_s[fg // orbs, lax.rem(fg, orbs)] + info_s[sg // orbs, lax.rem(sg, orbs)]
-        inverse = 1.0 / (levels + levels.T - occ)
-        t = c * (2.0 * c - c.T) * inverse
-        norm = -1.0 / (width * width)
-        e0 = jnp.sum(t) * norm
-        e1 = jnp.sum(t * inverse) * norm
-        fp_ref[j] = fp
-        sp_ref[j] = sp
-        c_ref[j] = c
-        here = lane == p
-        e_ref[0:1, :] = jnp.where(here, e0, e_ref[0:1, :])
-        e_ref[1:2, :] = jnp.where(here, e1, e_ref[1:2, :])
-        e_ref[2:3, :] = jnp.where(here, fg.astype(F32), e_ref[2:3, :])
-        e_ref[3:4, :] = jnp.where(here, sg.astype(F32), e_ref[3:4, :])
+    )(first_local, fetch_local, row_pair, x, pno, levels.reshape(pairs, 1, width), info)
 
 
 def group_of(pairs):
     return next(g for g in (4, 3, 2, 1) if pairs % g == 0)
-
-
-def coulomb_call(first_local, second, first_glob, info, x, gathered, pno, levels):
-    pairs, width, nvirt = pno.shape
-    aux = x.shape[2]
-    group = group_of(pairs)
-
-    def second_map(j, i, fl, sg, fg):
-        return (sg[i * group + j], 0, 0)
-
-    three = lambda i, *_: (i, 0, 0)
-    zero3 = lambda i, *_: (0, 0, 0)
-    return pl.pallas_call(
-        functools.partial(coulomb_kernel, group, x.shape[0]),
-        name="coulomb",
-        out_shape=(
-            jax.ShapeDtypeStruct((pairs, width, aux), BF16),
-            jax.ShapeDtypeStruct((pairs, width, aux), BF16),
-            jax.ShapeDtypeStruct((pairs, width, width), F32),
-            jax.ShapeDtypeStruct((8, 128), F32),
-        ),
-        grid_spec=pltpu.PrefetchScalarGridSpec(
-            num_scalar_prefetch=3,
-            grid=(pairs // group,),
-            in_specs=[
-                pl.BlockSpec(memory_space=pltpu.SMEM),
-                pl.BlockSpec(x.shape, zero3),
-                pl.BlockSpec((group, width, nvirt), three),
-                pl.BlockSpec((1, group, width), three),
-            ] + [pl.BlockSpec((1, nvirt, aux), functools.partial(second_map, j)) for j in range(group)],
-            out_specs=(
-                pl.BlockSpec((group, width, aux), three),
-                pl.BlockSpec((group, width, aux), three),
-                pl.BlockSpec((group, width, width), three),
-                pl.BlockSpec((8, 128), lambda i, *_: (0, 0)),
-            ),
-        ),
-        compiler_params=pltpu.CompilerParams(vmem_limit_bytes=VMEM_LIMIT),
-    )(first_local, second, first_glob, info, x, pno, levels.reshape(pairs // group, group, width), *([gathered] * group))
 
 
 def shift_kernel(n, orb_total, e_ref, out_ref, got, send, recv):
@@ -251,12 +294,13 @@
     )(energies)
 
 
-def density_kernel(group, orbs, first_s, slot_s, second_s, fglob_s, fresh_s, final_s, seen_s,
-                   info_s, shift_s, pno_ref, level_ref, fp_ref, sp_ref, c_ref,
-                   amp_ref, dens_ref, terms_ref, acc, stage, blank, busy, stage_sem, blank_sem):
+def density_kernel(group, orbs, first_s, slot_s, second_s, fglob_s, fresh_s, final_s, seen_s, row_s,
+                   info_s, shift_s, pno_ref, level_ref, *rest):
+    fp_refs, sp_refs, c_refs = rest[:group], rest[group:2 * group], rest[2 * group:3 * group]
+    amp_ref, dens_ref, terms_ref, acc, stage, blank, busy, stage_sem, blank_sem = rest[3 * group:]
     step = pl.program_id(0)
     width = pno_ref.shape[1]
-    aux = fp_ref.shape[2]
+    aux = fp_refs[0].shape[2]
     total = terms_ref.shape[0]
 
     def blank_copy(o):
@@ -281,12 +325,12 @@
         levels = jnp.broadcast_to(level_ref[0, j:j + 1, :], (width, width))
         occ = info_s[fg // orbs, lax.rem(fg, orbs)] + info_s[sg // orbs, lax.rem(sg, orbs)]
         inverse = 1.0 / (levels + levels.T - occ)
-        s1, s2 = shift_s[0, p], shift_s[1, p]
-        amp = -c_ref[j] * inverse * (1.0 - s2 * inverse * (1.0 - s1 * inverse))
+        s1, s2 = shift_s[0, row_s[p]], shift_s[1, row_s[p]]
+        amp = -c_refs[j][0] * inverse * (1.0 - s2 * inverse * (1.0 - s1 * inverse))
         amp_ref[j] = amp
         half = amp.astype(BF16)
-        part1 = jnp.dot(half, sp_ref[j], preferred_element_type=F32).astype(BF16)
-        part2 = lax.dot_general(half, fp_ref[j], (((0,), (0,)), ((), ())), preferred_element_type=F32).astype(BF16)
+        part1 = jnp.dot(half, sp_refs[j][0], preferred_element_type=F32).astype(BF16)
+        part2 = lax.dot_general(half, fp_refs[j][0], (((0,), (0,)), ((), ())), preferred_element_type=F32).astype(BF16)
         parts = jnp.concatenate([part1, part2], axis=1)
         pao = lax.dot_general(pno_ref[j], parts, (((0,), (0,)), ((), ())), preferred_element_type=F32)
         dens_ref[first_s[p]] += pao[:, :aux]
@@ -324,6 +368,13 @@
     aux = fp.shape[2]
     group = group_of(pairs)
     three = lambda i, *_: (i, 0, 0)
+
+    def row_map(j, i, *scalars):
+        return (scalars[-1][i * group + j], 0, 0)
+
+    def picked(array):
+        return [pl.BlockSpec((1,) + array.shape[1:], functools.partial(row_map, j)) for j in range(group)]
+
     smem = pl.BlockSpec(memory_space=pltpu.SMEM)
     dma = pltpu.SemaphoreType.DMA
     return pl.pallas_call(
@@ -335,16 +386,13 @@
             jax.ShapeDtypeStruct((orb_total, nvirt, aux), BF16),
         ),
         grid_spec=pltpu.PrefetchScalarGridSpec(
-            num_scalar_prefetch=7,
+            num_scalar_prefetch=8,
             grid=(pairs // group,),
             in_specs=[
                 smem, smem,
                 pl.BlockSpec((group, width, nvirt), three),
                 pl.BlockSpec((1, group, width), three),
-                pl.BlockSpec((group, width, aux), three),
-                pl.BlockSpec((group, width, aux), three),
-                pl.BlockSpec((group, width, width), three),
-            ],
+            ] + picked(fp) + picked(sp) + picked(c),
             out_specs=(
                 pl.BlockSpec((group, width, width), three),
                 pl.BlockSpec((orbs, nvirt, aux), lambda i, *_: (0, 0, 0)),
@@ -359,7 +407,7 @@
             ],
         ),
         compiler_params=pltpu.CompilerParams(vmem_limit_bytes=VMEM_LIMIT),
-    )(*scalars, info, shifts, pno, levels.reshape(pairs // group, group, width), fp, sp, c)
+    )(*scalars, info, shifts, pno, levels.reshape(pairs // group, group, width), *([fp] * group + [sp] * group + [c] * group))
 
 
 def home_kernel(n, terms_ref, dens_ref, out_ref, own, side, got, own_sem, side_send, side_recv, ring_send, ring_recv):
@@ -463,13 +511,16 @@
     final = 1 - jnp.any(same & (pair_ids[None, :] > pair_ids[:, None]), axis=1).astype(jnp.int32)
     seen = jnp.any(second[:, None] == jnp.arange(orb_total, dtype=jnp.int32)[None, :], axis=0).astype(jnp.int32)
     info = jnp.pad(occ_levels[None, :], ((0, 7), (0, 128 - orbs)))
-    gathered, info_all = gather(n, orb_blocks, info)
+    rank = jnp.sum((same & (pair_ids[None, :] < pair_ids[:, None])).astype(jnp.int32), axis=1)
+    row_of = slot_of * MOST + rank
+    row_ids = jnp.arange(slots * MOST, dtype=jnp.int32)
+    row_pair = jnp.max(jnp.where(row_of[None, :] == row_ids[:, None], pair_ids[None, :], -1), axis=1)
+    fp, sp, coulomb, energies, info_all = gather(
+        n, pair_i_local, fetch_local, row_pair, orb_blocks, pno, pno_levels, info
+    )
     info_all = info_all[:, 0, :orbs]
-    fp, sp, coulomb, energies = coulomb_call(
-        pair_i_local, second, first_glob, info_all, orb_blocks, gathered, pno, pno_levels
-    )
     shifts = shift_call(n, orb_total, energies)
-    scalars = (pair_i_local, slot_of, second, first_glob, fresh, final, seen)
+    scalars = (pair_i_local, slot_of, second, first_glob, fresh, final, seen, row_of)
     amplitude, density, terms = density_call(
         scalars, info_all, shifts, orbs, slots, orb_total, pno, pno_levels, fp, sp, coulomb
     )

time: 266 us -> 259 us (0.974)
  Pallas kernels: 251 us -> 240 us
    pallas_call x2 -> x1, Pallas kernels: 116 us -> 102 us  [gather(): pl.pallas_call(functools.partial(gather_kernel, n, per_owner), name='gath...]
where the time goes in v2:
time: 259 us; the launch traced here: 256 us
  Pallas kernels  240 us (93%)
  local copies, waits for them, and re-layouts  8.67 us (3%)
  other arithmetic  6.44 us (2%)
    pallas_call x1, Pallas kernels, gather(): pl.pallas_call(functools.partial(gather_kernel, n, per_owner), name='gath...  102 us
    pallas_call x1, Pallas kernels, home(): pl.pallas_call(functools.partial(home_kernel, n), name='terms_home', out_...  89.2 us
    pallas_call x1, Pallas kernels, density_call(): pl.pallas_call(functools.partial(density_kernel, group, orbs), name='dens...  40.4 us
    pallas_call x1, Pallas kernels, shift_call(): pl.pallas_call(functools.partial(shift_kernel, n, orb_total), name='shift...  8.28 us

profile of v2, /device:TPU:15, one launch (start us, length us, event | category | flops | bytes accessed | tf_op | source)
XLA Modules:
  0.0 256.1 jit_solution(2799075103721949293)
XLA Ops:
  0.6 0.7 fusion.4
  1.3 0.7 select_reduce_fusion.1.second_s
  2.0 0.0 copy-start.1
  2.0 0.1 fusion.1
  2.1 0.6 convert_element_type.16.seen_s
  2.7 0.9 convert_reduce_fusion
  3.6 1.3 multiply_add_fusion
  4.9 0.0 copy-start
  4.9 0.7 select_reduce_fusion.row_s
  5.6 0.9 fusion
  6.5 0.6 convert_subtract_fusion
  7.1 1.3 pad.4.info_ref
  8.3 1.4 reshape.22.level_ref
  9.8 1.5 reshape.21.level_ref
  11.2 102.4 %gather_coulomb.1 = (bf16[96,200,512]{2,1,0:T(8,128)(2,1)}, bf16[96,200,512]{2,1,0:T(8,128)(2,1)}, f32[96,200,200]{2,1,0:T(8,128)}, f32[8,128]{1,0:T(8,128)}, f32[16,8,128]{2,1,0:T(8,128)}) custom-call(s32[48]{0:T(128)} %first_s.3, s32[32]{0:T(128)} %fetch_s.1, s32[96]{0:T(128)} %select_reduce_fusion.row_s, bf16[4,256,512]{2,1,0:T(8,128)(2,1)} %x_ref.1, ...), custom_call_target="tpu_custom_call" | custom-call | tf_op jit(solution)/shard_map/gather_coulomb/pallas_call | solution.py:220
  113.6 1.4 slice.3
  115.1 8.3 %shifts.1.shift_s = f32[8,128]{1,0:T(8,128)} custom-call(f32[8,128]{1,0:T(8,128)} %get-tuple-element.11.e_ref), custom_call_target="tpu_custom_call" | custom-call | tf_op jit(solution)/shard_map/shifts/pallas_call | solution.py:286
  123.4 0.0 copy-done.1
  123.4 0.0 copy-done
  123.4 40.4 %density_terms.1 = (f32[48,200,200]{2,1,0:T(8,128)}, f32[4,256,512]{2,1,0:T(8,128)}, bf16[64,256,512]{2,1,0:T(8,128)(2,1)}) custom-call(s32[48]{0:T(128)} %first_s.3, s32[48]{0:T(128)} %bitcast.8, s32[48]{0:T(128)} %copy-done.1, s32[48]{0:T(128)} %get-tuple-element.23.fglob_s, s32[48]{0:T(128)} %get-tuple-element.21.fresh_s, s32[48]{0:T(128)} %get-tuple-element.20.final_s, ...), custom_call_target="tpu_custom_call" | custom-call | tf_op jit(solution)/shard_map/density_terms/pallas_call | solution.py:380
  163.8 89.2 %terms_home.1 = f32[4,256,512]{2,1,0:T(8,128)} custom-call(bf16[64,256,512]{2,1,0:T(8,128)(2,1)} %get-tuple-element.16.terms_ref, f32[4,256,512]{2,1,0:T(8,128)} %get-tuple-element.17.dens_ref), custom_call_target="tpu_custom_call" | custom-call | tf_op jit(solution)/shard_map/terms_home/pallas_call | solution.py:480
  253.0 3.1 %copy.15 = f32[4,256,512]{2,1,0:T(8,128)} copy(f32[4,256,512]{2,1,0:T(8,128)} %terms_home.1) | data formatting | bytes 4194304
Async XLA Ops:
  2.0 121.3 %copy-start.1 = (s32[48]{0:T(128)}, s32[48]{0:T(128)S(1)}, u32[]{:S(2)}) copy-start(s32[48]{0:T(128)S(1)} %select_reduce_fusion.1.second_s) | copy-start | bytes 580
  4.9 118.5 %copy-start = (s32[48]{0:T(128)}, s32[48]{0:T(128)S(1)}, u32[]{:S(2)}) copy-start(s32[48]{0:T(128)S(1)} %get-tuple-element.22.row_s) | copy-start | bytes 580

commit v3 on v2

--- a/solution.py
+++ b/solution.py
@@ -59,7 +59,7 @@
 
 def gather_kernel(n, per_owner, first_s, fetch_s, row_s, x_ref, pno_ref, level_ref, info_ref,
                   fp_out, sp_out, c_out, e_ref, info_out,
-                  blocks, current, fp_stage, sp_stage, c_stage,
+                  blocks, moments, fp_stage, sp_stage, c_stage,
                   own_sem, first_send, first_recv, ring_send, ring_recv, side_send, side_recv, info_send, info_recv, out_sem):
     me, chips, core, place, dev = ring(n)
     orbs = x_ref.shape[0]
@@ -113,36 +113,39 @@
             block = blocks[owner, 0]
             for other in range(1, orbs):
                 block = jnp.where(local == other, blocks[owner, other], block)
-            current[...] = block
             occ2 = jnp.sum(jnp.where(lane == local, info_out[owner, 0:1, :], 0.0), axis=1, keepdims=True)
+            base = owner * rows + s * MOST
+            named = [row_s[base + m] for m in range(MOST)]
+            pair = [jnp.maximum(q, 0) for q in named]
+            first = [first_s[q] for q in pair]
+            w = [pno_ref[q] for q in pair]
+            inverse = []
+            for m in range(MOST):
+                levels = jnp.broadcast_to(level_ref[pair[m]], (width, width))
+                occ1 = jnp.sum(jnp.where(lane == first[m], info_ref[0:1, :], 0.0), axis=1, keepdims=True)
+                inverse.append(1.0 / (levels + levels.T - (occ1 + occ2)))
+            sp = [jnp.dot(w[m], block, preferred_element_type=F32).astype(BF16) for m in range(MOST)]
+            fp = [jnp.dot(w[m], x_ref[first[m]], preferred_element_type=F32).astype(BF16) for m in range(MOST)]
+            c = [
+                lax.dot_general(fp[m], sp[m], (((1,), (1,)), ((), ())), preferred_element_type=F32) * scale
+                for m in range(MOST)
+            ]
+            t = [c[m] * (2.0 * c[m] - c[m].T) * inverse[m] for m in range(MOST)]
             for m in range(MOST):
                 i = s * MOST + m
-                row = owner * rows + i
-                named = row_s[row]
-                q = jnp.maximum(named, 0)
-                first = first_s[q]
-                w = pno_ref[q]
-                fp = jnp.dot(w, x_ref[first], preferred_element_type=F32).astype(BF16)
-                sp = jnp.dot(w, current[...], preferred_element_type=F32).astype(BF16)
-                c = lax.dot_general(fp, sp, (((1,), (1,)), ((), ())), preferred_element_type=F32) * scale
-                levels = jnp.broadcast_to(level_ref[q], (width, width))
-                occ1 = jnp.sum(jnp.where(lane == first, info_ref[0:1, :], 0.0), axis=1, keepdims=True)
-                inverse = 1.0 / (levels + levels.T - (occ1 + occ2))
-                t = c * (2.0 * c - c.T) * inverse
-                e0 = jnp.sum(t) * norm
-                e1 = jnp.sum(t * inverse) * norm
-                fp_stage[way, i] = fp
-                sp_stage[way, i] = sp
-                c_stage[way, i] = c
-                for copy in out_copies(way, owner, i):
-                    copy.start()
-                here = lane == row
-                id1 = jnp.where(named >= 0, me * orbs + first, -1).astype(F32)
-                id2 = jnp.where(named >= 0, owner * orbs + local, -1).astype(F32)
-                e_ref[0:1, :] = jnp.where(here, e0, e_ref[0:1, :])
-                e_ref[1:2, :] = jnp.where(here, e1, e_ref[1:2, :])
+                fp_stage[way, i] = fp[m]
+                sp_stage[way, i] = sp[m]
+                c_stage[way, i] = c[m]
+                moments[0, pl.ds(base + m, 1), :] = jnp.sum(t[m], axis=0, keepdims=True)
+                moments[1, pl.ds(base + m, 1), :] = jnp.sum(t[m] * inverse[m], axis=0, keepdims=True)
+                here = lane == base + m
+                id1 = jnp.where(named[m] >= 0, me * orbs + first[m], -1).astype(F32)
+                id2 = jnp.where(named[m] >= 0, owner * orbs + local, -1).astype(F32)
                 e_ref[2:3, :] = jnp.where(here, id1, e_ref[2:3, :])
                 e_ref[3:4, :] = jnp.where(here, id2, e_ref[3:4, :])
+        for i in range(rows):
+            for copy in out_copies(way, owner, i):
+                copy.start()
 
     for k in range(orbs):
         first_copy(k).start()
@@ -159,6 +162,7 @@
     info_out[me] = info_ref[...]
     e_ref[...] = jnp.zeros_like(e_ref)
     e_ref[2:4, :] = jnp.full((2, 128), -1.0, F32)
+    moments[...] = jnp.zeros_like(moments)
     for k in range(half, orbs):
         first_copy(k).wait_recv()
     for d in range(1, n):
@@ -191,6 +195,10 @@
         return carry
 
     lax.fori_loop(1, chips + 1, turn, 0)
+    square = lax.broadcasted_iota(jnp.int32, (128, 128), 0) == lax.broadcasted_iota(jnp.int32, (128, 128), 1)
+    for kind in range(2):
+        column = jnp.sum(moments[kind], axis=1, keepdims=True) * norm
+        e_ref[kind:kind + 1, :] = jnp.sum(jnp.where(square, column, 0.0), axis=0, keepdims=True)
     for way in range(2):
         for i in range(rows):
             for copy in out_copies(way, owner_at(way, chips - 1), i):
@@ -231,7 +239,7 @@
         out_specs=(anywhere, anywhere, anywhere, vmem, vmem),
         scratch_shapes=[
             pltpu.VMEM((n, orbs, nvirt, aux), BF16),
-            pltpu.VMEM((nvirt, aux), BF16),
+            pltpu.VMEM((2, 128, width), F32),
             pltpu.VMEM((2, rows, width, aux), BF16),
             pltpu.VMEM((2, rows, width, aux), BF16),
             pltpu.VMEM((2, rows, width, width), F32),
@@ -319,23 +327,33 @@
             def _():
                 blank_copy(o).start()
 
+    halves = []
     for j in range(group):
         p = step * group + j
-        fg, sg, slot = fglob_s[p], second_s[p], slot_s[p]
+        fg, sg = fglob_s[p], second_s[p]
         levels = jnp.broadcast_to(level_ref[0, j:j + 1, :], (width, width))
         occ = info_s[fg // orbs, lax.rem(fg, orbs)] + info_s[sg // orbs, lax.rem(sg, orbs)]
         inverse = 1.0 / (levels + levels.T - occ)
         s1, s2 = shift_s[0, row_s[p]], shift_s[1, row_s[p]]
         amp = -c_refs[j][0] * inverse * (1.0 - s2 * inverse * (1.0 - s1 * inverse))
         amp_ref[j] = amp
-        half = amp.astype(BF16)
-        part1 = jnp.dot(half, sp_refs[j][0], preferred_element_type=F32).astype(BF16)
-        part2 = lax.dot_general(half, fp_refs[j][0], (((0,), (0,)), ((), ())), preferred_element_type=F32).astype(BF16)
-        parts = jnp.concatenate([part1, part2], axis=1)
-        pao = lax.dot_general(pno_ref[j], parts, (((0,), (0,)), ((), ())), preferred_element_type=F32)
+        halves.append(amp.astype(BF16))
+    parts = []
+    for j in range(group):
+        part1 = jnp.dot(halves[j], sp_refs[j][0], preferred_element_type=F32).astype(BF16)
+        part2 = lax.dot_general(halves[j], fp_refs[j][0], (((0,), (0,)), ((), ())), preferred_element_type=F32).astype(BF16)
+        parts.append(jnp.concatenate([part1, part2], axis=1))
+    for j in range(group):
+        p = step * group + j
+        slot = slot_s[p]
+        pao = lax.dot_general(pno_ref[j], parts[j], (((0,), (0,)), ((), ())), preferred_element_type=F32)
         dens_ref[first_s[p]] += pao[:, :aux]
         term = pao[:, aux:]
         acc[slot] = jnp.where(fresh_s[p] == 1, term, acc[slot] + term)
+
+    for j in range(group):
+        p = step * group + j
+        sg, slot = second_s[p], slot_s[p]
 
         @pl.when(final_s[p] == 1)
         def _():

time: 259 us -> 248 us (0.958)
  Pallas kernels: 240 us -> 229 us
    pallas_call x1, Pallas kernels: 40.4 us -> 31.1 us  [density_call(): pl.pallas_call(functools.partial(density_kernel, group, orbs), name='dens...]
where the time goes in v3:
time: 248 us; the launch traced here: 245 us
  Pallas kernels  229 us (92%)
  local copies, waits for them, and re-layouts  8.67 us (3%)
  other arithmetic  6.44 us (3%)
    pallas_call x1, Pallas kernels, gather(): pl.pallas_call(functools.partial(gather_kernel, n, per_owner), name='gath...  102 us
    pallas_call x1, Pallas kernels, home(): pl.pallas_call(functools.partial(home_kernel, n), name='terms_home', out_...  88.5 us
    pallas_call x1, Pallas kernels, density_call(): pl.pallas_call(functools.partial(density_kernel, group, orbs), name='dens...  31.1 us
    pallas_call x1, Pallas kernels, shift_call(): pl.pallas_call(functools.partial(shift_kernel, n, orb_total), name='shift...  8.05 us

profile of v3, /device:TPU:15, one launch (start us, length us, event | category | flops | bytes accessed | tf_op | source)
XLA Modules:
  0.0 245.0 jit_solution(928634970668618706)
XLA Ops:
  0.6 0.7 fusion.4
  1.3 0.7 select_reduce_fusion.1.second_s
  2.0 0.0 copy-start.1
  2.0 0.1 fusion.1
  2.1 0.6 convert_element_type.16.seen_s
  2.7 0.9 convert_reduce_fusion
  3.6 1.3 multiply_add_fusion
  4.9 0.0 copy-start
  4.9 0.7 select_reduce_fusion.row_s
  5.6 0.9 fusion
  6.5 0.6 convert_subtract_fusion
  7.1 1.3 pad.4.info_ref
  8.3 1.4 reshape.22.level_ref
  9.8 1.5 reshape.21.level_ref
  11.2 101.5 %gather_coulomb.1 = (bf16[96,200,512]{2,1,0:T(8,128)(2,1)}, bf16[96,200,512]{2,1,0:T(8,128)(2,1)}, f32[96,200,200]{2,1,0:T(8,128)}, f32[8,128]{1,0:T(8,128)}, f32[16,8,128]{2,1,0:T(8,128)}) custom-call(s32[48]{0:T(128)} %first_s.3, s32[32]{0:T(128)} %fetch_s.1, s32[96]{0:T(128)} %select_reduce_fusion.row_s, bf16[4,256,512]{2,1,0:T(8,128)(2,1)} %x_ref.1, ...), custom_call_target="tpu_custom_call" | custom-call | tf_op jit(solution)/shard_map/gather_coulomb/pallas_call | solution.py:228
  112.7 1.4 slice.3
  114.2 8.1 %shifts.1.shift_s = f32[8,128]{1,0:T(8,128)} custom-call(f32[8,128]{1,0:T(8,128)} %get-tuple-element.11.e_ref), custom_call_target="tpu_custom_call" | custom-call | tf_op jit(solution)/shard_map/shifts/pallas_call | solution.py:294
  122.2 0.0 copy-done.1
  122.3 0.0 copy-done
  122.3 31.1 %density_terms.1 = (f32[48,200,200]{2,1,0:T(8,128)}, f32[4,256,512]{2,1,0:T(8,128)}, bf16[64,256,512]{2,1,0:T(8,128)(2,1)}) custom-call(s32[48]{0:T(128)} %first_s.3, s32[48]{0:T(128)} %bitcast.8, s32[48]{0:T(128)} %copy-done.1, s32[48]{0:T(128)} %get-tuple-element.23.fglob_s, s32[48]{0:T(128)} %get-tuple-element.21.fresh_s, s32[48]{0:T(128)} %get-tuple-element.20.final_s, ...), custom_call_target="tpu_custom_call" | custom-call | tf_op jit(solution)/shard_map/density_terms/pallas_call | solution.py:398
  153.4 88.5 %terms_home.1 = f32[4,256,512]{2,1,0:T(8,128)} custom-call(bf16[64,256,512]{2,1,0:T(8,128)(2,1)} %get-tuple-element.16.terms_ref, f32[4,256,512]{2,1,0:T(8,128)} %get-tuple-element.17.dens_ref), custom_call_target="tpu_custom_call" | custom-call | tf_op jit(solution)/shard_map/terms_home/pallas_call | solution.py:498
  241.9 3.1 %copy.15 = f32[4,256,512]{2,1,0:T(8,128)} copy(f32[4,256,512]{2,1,0:T(8,128)} %terms_home.1) | data formatting | bytes 4194304
Async XLA Ops:
  2.0 120.2 %copy-start.1 = (s32[48]{0:T(128)}, s32[48]{0:T(128)S(1)}, u32[]{:S(2)}) copy-start(s32[48]{0:T(128)S(1)} %select_reduce_fusion.1.second_s) | copy-start | bytes 580
  4.9 117.4 %copy-start = (s32[48]{0:T(128)}, s32[48]{0:T(128)S(1)}, u32[]{:S(2)}) copy-start(s32[48]{0:T(128)S(1)} %get-tuple-element.22.row_s) | copy-start | bytes 580

commit v4 on v3

--- a/solution.py
+++ b/solution.py
@@ -57,10 +57,35 @@
     )
 
 
-def gather_kernel(n, per_owner, first_s, fetch_s, row_s, x_ref, pno_ref, level_ref, info_ref,
-                  fp_out, sp_out, c_out, e_ref, info_out,
-                  blocks, moments, fp_stage, sp_stage, c_stage,
-                  own_sem, first_send, first_recv, ring_send, ring_recv, side_send, side_recv, info_send, info_recv, out_sem):
+def shifts(n, orb_total, e_ref, got, out_ref):
+    ids = lax.broadcasted_iota(jnp.int32, (orb_total, 128), 0).astype(F32)
+
+    def shares(block):
+        return jnp.where(ids == block[2:3, :], 1.0, 0.0) + jnp.where(ids == block[3:4, :], 1.0, 0.0)
+
+    total = jnp.zeros((orb_total, 128), F32)
+    for d in range(n):
+        block = got[d]
+        total = total + shares(block) * block[0:1, :]
+    shift = shift_weight * jnp.sum(total, axis=1, keepdims=True)
+    total = jnp.zeros((orb_total, 128), F32)
+    for d in range(n):
+        block = got[d]
+        hot = shares(block)
+        pair_shift = jnp.sum(hot * shift, axis=0, keepdims=True)
+        total = total + hot * (block[0:1, :] - pair_shift * block[1:2, :])
+    shift2 = shift_weight * jnp.sum(total, axis=1, keepdims=True)
+    mine = shares(e_ref[...])
+    out_ref[...] = jnp.zeros_like(out_ref)
+    out_ref[0:1, :] = jnp.sum(mine * shift, axis=0, keepdims=True)
+    out_ref[1:2, :] = jnp.sum(mine * shift2, axis=0, keepdims=True)
+    out_ref[2:3, :] = e_ref[4:5, :]
+
+
+def gather_kernel(n, per_owner, first_s, fetch_s, row_s, occ_s, x_ref, pno_in, level_ref,
+                  fp_out, sp_out, c_out, shift_ref,
+                  pno_ref, info_ref, info_out, e_ref, got, blocks, moments, fp_stage, sp_stage, c_stage,
+                  own_sem, first_send, first_recv, ring_send, ring_recv, side_send, side_recv, info_send, info_recv, e_send, e_recv, out_sem):
     me, chips, core, place, dev = ring(n)
     orbs = x_ref.shape[0]
     half = orbs // 2
@@ -71,6 +96,12 @@
     sibling = me + 1 - 2 * core
     ends = (dev(place + 1, core), dev(place - 1, core))
     lane = lax.broadcasted_iota(jnp.int32, (1, 128), 1)
+    pno_copy = pltpu.make_async_copy(pno_in, pno_ref, own_sem.at[1])
+    pno_copy.start()
+    levels_row = jnp.zeros((8, 128), F32)
+    for l in range(orbs):
+        levels_row = jnp.where(lane == l, occ_s[l], levels_row)
+    info_ref[...] = levels_row
     greet([lax.rem(me + d, n) for d in range(1, n)])
 
     def owner_at(way, step):
@@ -119,11 +150,12 @@
             pair = [jnp.maximum(q, 0) for q in named]
             first = [first_s[q] for q in pair]
             w = [pno_ref[q] for q in pair]
-            inverse = []
+            inverse, occ = [], []
             for m in range(MOST):
-                levels = jnp.broadcast_to(level_ref[pair[m]], (width, width))
+                levels = jnp.broadcast_to(level_ref[pl.ds(pair[m], 1), :], (width, width))
                 occ1 = jnp.sum(jnp.where(lane == first[m], info_ref[0:1, :], 0.0), axis=1, keepdims=True)
-                inverse.append(1.0 / (levels + levels.T - (occ1 + occ2)))
+                occ.append(occ1 + occ2)
+                inverse.append(1.0 / (levels + levels.T - occ[m]))
             sp = [jnp.dot(w[m], block, preferred_element_type=F32).astype(BF16) for m in range(MOST)]
             fp = [jnp.dot(w[m], x_ref[first[m]], preferred_element_type=F32).astype(BF16) for m in range(MOST)]
             c = [
@@ -143,6 +175,7 @@
                 id2 = jnp.where(named[m] >= 0, owner * orbs + local, -1).astype(F32)
                 e_ref[2:3, :] = jnp.where(here, id1, e_ref[2:3, :])
                 e_ref[3:4, :] = jnp.where(here, id2, e_ref[3:4, :])
+                e_ref[4:5, :] = jnp.where(here, occ[m], e_ref[4:5, :])
         for i in range(rows):
             for copy in out_copies(way, owner, i):
                 copy.start()
@@ -167,6 +200,7 @@
         first_copy(k).wait_recv()
     for d in range(1, n):
         note(d).wait()
+    pno_copy.wait()
 
     def turn(step, carry):
         for k in range(half):
@@ -199,6 +233,16 @@
     for kind in range(2):
         column = jnp.sum(moments[kind], axis=1, keepdims=True) * norm
         e_ref[kind:kind + 1, :] = jnp.sum(jnp.where(square, column, 0.0), axis=0, keepdims=True)
+
+    def energy_copy(d):
+        return remote(e_ref, got.at[me], e_send.at[d - 1], e_recv.at[d - 1], lax.rem(me + d, n))
+
+    for d in range(1, n):
+        energy_copy(d).start()
+    got[me] = e_ref[...]
+    for d in range(1, n):
+        energy_copy(d).wait()
+    shifts(n, n * orbs, e_ref, got, shift_ref)
     for way in range(2):
         for i in range(rows):
             for copy in out_copies(way, owner_at(way, chips - 1), i):
@@ -216,7 +260,7 @@
     lax.fori_loop(1, chips, drain, 0)
 
 
-def gather(n, first_local, fetch_local, row_pair, x, pno, levels, info):
+def gather(n, first_local, fetch_local, row_pair, occ, x, pno, levels):
     pairs, width, nvirt = pno.shape
     orbs, _, aux = x.shape
     per_owner = fetch_local.shape[0] // n
@@ -233,77 +277,34 @@
             jax.ShapeDtypeStruct((total, width, aux), BF16),
             jax.ShapeDtypeStruct((total, width, width), F32),
             jax.ShapeDtypeStruct((8, 128), F32),
-            jax.ShapeDtypeStruct((n,) + info.shape, info.dtype),
         ),
-        in_specs=[smem, smem, smem, vmem, vmem, vmem, vmem],
-        out_specs=(anywhere, anywhere, anywhere, vmem, vmem),
+        in_specs=[smem, smem, smem, smem, vmem, anywhere, vmem],
+        out_specs=(anywhere, anywhere, anywhere, vmem),
         scratch_shapes=[
+            pltpu.VMEM(pno.shape, BF16),
+            pltpu.VMEM((8, 128), F32),
+            pltpu.VMEM((n, 8, 128), F32),
+            pltpu.VMEM((8, 128), F32),
+            pltpu.VMEM((n, 8, 128), F32),
             pltpu.VMEM((n, orbs, nvirt, aux), BF16),
             pltpu.VMEM((2, 128, width), F32),
             pltpu.VMEM((2, rows, width, aux), BF16),
             pltpu.VMEM((2, rows, width, aux), BF16),
             pltpu.VMEM((2, rows, width, width), F32),
-            dma((1,)), dma((orbs,)), dma((orbs,)),
+            dma((2,)), dma((orbs,)), dma((orbs,)),
             dma((2, chips, half)), dma((2, chips, half)), dma((2, chips, half)), dma((2, chips, half)),
-            dma((n - 1,)), dma((n - 1,)), dma((2, 3, rows)),
+            dma((n - 1,)), dma((n - 1,)), dma((n - 1,)), dma((n - 1,)), dma((2, 3, rows)),
         ],
         compiler_params=pltpu.CompilerParams(collective_id=0, has_side_effects=True, vmem_limit_bytes=VMEM_LIMIT),
-    )(first_local, fetch_local, row_pair, x, pno, levels.reshape(pairs, 1, width), info)
+    )(first_local, fetch_local, row_pair, occ, x, pno, levels)
 
 
 def group_of(pairs):
     return next(g for g in (4, 3, 2, 1) if pairs % g == 0)
 
 
-def shift_kernel(n, orb_total, e_ref, out_ref, got, send, recv):
-    me = lax.axis_index("orb")
-    greet([lax.rem(me + d, n) for d in range(1, n)])
-    copies = []
-    for d in range(1, n):
-        copy = remote(e_ref, got.at[me], send.at[d - 1], recv.at[d - 1], lax.rem(me + d, n))
-        copy.start()
-        copies.append(copy)
-    got[me] = e_ref[...]
-    for copy in copies:
-        copy.wait()
-    ids = lax.broadcasted_iota(jnp.int32, (orb_total, 128), 0).astype(F32)
-
-    def shares(block):
-        return jnp.where(ids == block[2:3, :], 1.0, 0.0) + jnp.where(ids == block[3:4, :], 1.0, 0.0)
-
-    total = jnp.zeros((orb_total, 128), F32)
-    for d in range(n):
-        block = got[d]
-        total = total + shares(block) * block[0:1, :]
-    shift = shift_weight * jnp.sum(total, axis=1, keepdims=True)
-    total = jnp.zeros((orb_total, 128), F32)
-    for d in range(n):
-        block = got[d]
-        hot = shares(block)
-        pair_shift = jnp.sum(hot * shift, axis=0, keepdims=True)
-        total = total + hot * (block[0:1, :] - pair_shift * block[1:2, :])
-    shift2 = shift_weight * jnp.sum(total, axis=1, keepdims=True)
-    mine = shares(e_ref[...])
-    out_ref[...] = jnp.zeros_like(out_ref)
-    out_ref[0:1, :] = jnp.sum(mine * shift, axis=0, keepdims=True)
-    out_ref[1:2, :] = jnp.sum(mine * shift2, axis=0, keepdims=True)
-
-
-def shift_call(n, orb_total, energies):
-    dma = pltpu.SemaphoreType.DMA
-    return pl.pallas_call(
-        functools.partial(shift_kernel, n, orb_total),
-        name="shifts",
-        out_shape=jax.ShapeDtypeStruct((8, 128), F32),
-        in_specs=[pl.BlockSpec(memory_space=pltpu.VMEM)],
-        out_specs=pl.BlockSpec(memory_space=pltpu.VMEM),
-        scratch_shapes=[pltpu.VMEM((n, 8, 128), F32), dma((n - 1,)), dma((n - 1,))],
-        compiler_params=pltpu.CompilerParams(collective_id=1, has_side_effects=True, vmem_limit_bytes=VMEM_LIMIT),
-    )(energies)
-
-
-def density_kernel(group, orbs, first_s, slot_s, second_s, fglob_s, fresh_s, final_s, seen_s, row_s,
-                   info_s, shift_s, pno_ref, level_ref, *rest):
+def density_kernel(group, first_s, slot_s, second_s, fresh_s, final_s, seen_s, row_s,
+                   shift_s, pno_ref, level_ref, *rest):
     fp_refs, sp_refs, c_refs = rest[:group], rest[group:2 * group], rest[2 * group:3 * group]
     amp_ref, dens_ref, terms_ref, acc, stage, blank, busy, stage_sem, blank_sem = rest[3 * group:]
     step = pl.program_id(0)
@@ -330,11 +331,9 @@
     halves = []
     for j in range(group):
         p = step * group + j
-        fg, sg = fglob_s[p], second_s[p]
-        levels = jnp.broadcast_to(level_ref[0, j:j + 1, :], (width, width))
-        occ = info_s[fg // orbs, lax.rem(fg, orbs)] + info_s[sg // orbs, lax.rem(sg, orbs)]
+        levels = jnp.broadcast_to(level_ref[pl.ds(p, 1), :], (width, width))
+        s1, s2, occ = shift_s[0, row_s[p]], shift_s[1, row_s[p]], shift_s[2, row_s[p]]
         inverse = 1.0 / (levels + levels.T - occ)
-        s1, s2 = shift_s[0, row_s[p]], shift_s[1, row_s[p]]
         amp = -c_refs[j][0] * inverse * (1.0 - s2 * inverse * (1.0 - s1 * inverse))
         amp_ref[j] = amp
         halves.append(amp.astype(BF16))
@@ -381,7 +380,7 @@
                 blank_copy(o).wait()
 
 
-def density_call(scalars, info, shifts, orbs, slots, orb_total, pno, levels, fp, sp, c):
+def density_call(scalars, shifts, orbs, slots, orb_total, pno, levels, fp, sp, c):
     pairs, width, nvirt = pno.shape
     aux = fp.shape[2]
     group = group_of(pairs)
@@ -396,7 +395,7 @@
     smem = pl.BlockSpec(memory_space=pltpu.SMEM)
     dma = pltpu.SemaphoreType.DMA
     return pl.pallas_call(
-        functools.partial(density_kernel, group, orbs),
+        functools.partial(density_kernel, group),
         name="density_terms",
         out_shape=(
             jax.ShapeDtypeStruct((pairs, width, width), F32),
@@ -404,12 +403,12 @@
             jax.ShapeDtypeStruct((orb_total, nvirt, aux), BF16),
         ),
         grid_spec=pltpu.PrefetchScalarGridSpec(
-            num_scalar_prefetch=8,
+            num_scalar_prefetch=7,
             grid=(pairs // group,),
             in_specs=[
-                smem, smem,
+                smem,
                 pl.BlockSpec((group, width, nvirt), three),
-                pl.BlockSpec((1, group, width), three),
+                pl.BlockSpec(levels.shape, lambda i, *_: (0, 0)),
             ] + picked(fp) + picked(sp) + picked(c),
             out_specs=(
                 pl.BlockSpec((group, width, width), three),
@@ -425,7 +424,7 @@
             ],
         ),
         compiler_params=pltpu.CompilerParams(vmem_limit_bytes=VMEM_LIMIT),
-    )(*scalars, info, shifts, pno, levels.reshape(pairs // group, group, width), *([fp] * group + [sp] * group + [c] * group))
+    )(*scalars, shifts, pno, levels, *([fp] * group + [sp] * group + [c] * group))
 
 
 def home_kernel(n, terms_ref, dens_ref, out_ref, own, side, got, own_sem, side_send, side_recv, ring_send, ring_recv):
@@ -522,25 +521,21 @@
     slot_ids = jnp.arange(slots, dtype=jnp.int32)
     pair_ids = jnp.arange(pairs, dtype=jnp.int32)
     slot_orb = slot_ids // per_owner * orbs + fetch_local
-    first_glob = lax.axis_index("orb") * orbs + pair_i_local
     second = jnp.sum(jnp.where(slot_of[:, None] == slot_ids[None, :], slot_orb[None, :], 0), axis=1)
     same = slot_of[:, None] == slot_of[None, :]
     fresh = 1 - jnp.any(same & (pair_ids[None, :] < pair_ids[:, None]), axis=1).astype(jnp.int32)
     final = 1 - jnp.any(same & (pair_ids[None, :] > pair_ids[:, None]), axis=1).astype(jnp.int32)
     seen = jnp.any(second[:, None] == jnp.arange(orb_total, dtype=jnp.int32)[None, :], axis=0).astype(jnp.int32)
-    info = jnp.pad(occ_levels[None, :], ((0, 7), (0, 128 - orbs)))
     rank = jnp.sum((same & (pair_ids[None, :] < pair_ids[:, None])).astype(jnp.int32), axis=1)
     row_of = slot_of * MOST + rank
     row_ids = jnp.arange(slots * MOST, dtype=jnp.int32)
     row_pair = jnp.max(jnp.where(row_of[None, :] == row_ids[:, None], pair_ids[None, :], -1), axis=1)
-    fp, sp, coulomb, energies, info_all = gather(
-        n, pair_i_local, fetch_local, row_pair, orb_blocks, pno, pno_levels, info
+    fp, sp, coulomb, pair_shifts = gather(
+        n, pair_i_local, fetch_local, row_pair, occ_levels, orb_blocks, pno, pno_levels
     )
-    info_all = info_all[:, 0, :orbs]
-    shifts = shift_call(n, orb_total, energies)
-    scalars = (pair_i_local, slot_of, second, first_glob, fresh, final, seen, row_of)
+    scalars = (pair_i_local, slot_of, second, fresh, final, seen, row_of)
     amplitude, density, terms = density_call(
-        scalars, info_all, shifts, orbs, slots, orb_total, pno, pno_levels, fp, sp, coulomb
+        scalars, pair_shifts, orbs, slots, orb_total, pno, pno_levels, fp, sp, coulomb
     )
     return (amplitude, home(n, terms, density))
 

time: 248 us -> 235 us (0.948)
  Pallas kernels: 229 us -> 223 us
  local copies, waits for them, and re-layouts: 8.67 us -> 3.09 us
    pallas_call x2 -> x1, Pallas kernels: 39.2 us -> 30.9 us  [density_call(): pl.pallas_call(functools.partial(density_kernel, group), name='density_te...]
    reshape x2 -> x0, local copies, waits for them, and re-layouts: 2.88 us -> none  [the longest x1 1.45 us: gather(): levels.reshape(pairs, 1, width)]
where the time goes in v4:
time: 235 us; the launch traced here: 233 us
  Pallas kernels  223 us (95%)
  other arithmetic  5.78 us (2%)
  local copies, waits for them, and re-layouts  3.09 us (1%)
    pallas_call x1, Pallas kernels, gather(): pl.pallas_call(functools.partial(gather_kernel, n, per_owner), name='gath...  104 us
    pallas_call x1, Pallas kernels, home(): pl.pallas_call(functools.partial(home_kernel, n), name='terms_home', out_...  88.4 us
    pallas_call x1, Pallas kernels, density_call(): pl.pallas_call(functools.partial(density_kernel, group), name='density_te...  30.9 us

profile of v4, /device:TPU:15, one launch (start us, length us, event | category | flops | bytes accessed | tf_op | source)
XLA Modules:
  0.0 232.6 jit_solution(1586739922230767737)
XLA Ops:
  0.6 0.7 fusion.4
  1.3 0.7 select_reduce_fusion.1.second_s
  2.0 0.0 copy-start
  2.0 0.1 fusion.1
  2.1 0.6 convert_element_type.14.seen_s
  2.7 0.9 convert_reduce_fusion
  3.6 0.7 multiply_add_fusion.row_s
  4.3 0.0 copy-start.1
  4.3 0.6 select_reduce_fusion.row_s
  4.9 0.9 fusion
  5.8 0.6 convert_subtract_fusion
  6.4 103.8 %gather_coulomb.1 = (bf16[96,200,512]{2,1,0:T(8,128)(2,1)}, bf16[96,200,512]{2,1,0:T(8,128)(2,1)}, f32[96,200,200]{2,1,0:T(8,128)}, f32[8,128]{1,0:T(8,128)}) custom-call(s32[48]{0:T(128)} %first_s.3, s32[32]{0:T(128)} %fetch_s.1, s32[96]{0:T(128)} %select_reduce_fusion.row_s, f32[4]{0:T(128)} %occ_s.1, bf16[4,256,512]{2,1,0:T(8,128)(2,1)} %x_ref.1, ...), custom_call_target="tpu_custom_call" | custom-call | tf_op jit(solution)/shard_map/gather_coulomb/pallas_call | solution.py:272
  110.3 0.0 copy-done
  110.3 0.0 copy-done.1
  110.3 30.9 %density_terms.1 = (f32[48,200,200]{2,1,0:T(8,128)}, f32[4,256,512]{2,1,0:T(8,128)}, bf16[64,256,512]{2,1,0:T(8,128)(2,1)}) custom-call(s32[48]{0:T(128)} %first_s.3, s32[48]{0:T(128)} %bitcast.5, s32[48]{0:T(128)} %copy-done, s32[48]{0:T(128)} %get-tuple-element.19.fresh_s, s32[48]{0:T(128)} %get-tuple-element.18.final_s, s32[64]{0:T(128)} %convert_element_type.14.seen_s, ...), custom_call_target="tpu_custom_call" | custom-call | tf_op jit(solution)/shard_map/density_terms/pallas_call | solution.py:397
  141.1 88.4 %terms_home.1 = f32[4,256,512]{2,1,0:T(8,128)} custom-call(bf16[64,256,512]{2,1,0:T(8,128)(2,1)} %get-tuple-element.14.terms_ref, f32[4,256,512]{2,1,0:T(8,128)} %get-tuple-element.15.dens_ref), custom_call_target="tpu_custom_call" | custom-call | tf_op jit(solution)/shard_map/terms_home/pallas_call | solution.py:497
  229.5 3.1 %copy.10 = f32[4,256,512]{2,1,0:T(8,128)} copy(f32[4,256,512]{2,1,0:T(8,128)} %terms_home.1) | data formatting | bytes 4194304
Async XLA Ops:
  2.0 108.2 %copy-start = (s32[48]{0:T(128)}, s32[48]{0:T(128)S(1)}, u32[]{:S(2)}) copy-start(s32[48]{0:T(128)S(1)} %select_reduce_fusion.1.second_s) | copy-start | bytes 580
  4.3 106.0 %copy-start.1 = (s32[48]{0:T(128)}, s32[48]{0:T(128)S(1)}, u32[]{:S(2)}) copy-start(s32[48]{0:T(128)S(1)} %multiply_add_fusion.row_s) | copy-start | bytes 580

commit v5 on v4

--- a/solution.py
+++ b/solution.py
@@ -204,17 +204,6 @@
 
     def turn(step, carry):
         for k in range(half):
-            @pl.when(step < chips)
-            def _():
-                for way in range(2):
-                    ring_wait(way, step, k)
-
-                    @pl.when(step < chips - 1)
-                    def _():
-                        ring_copy(way, step + 1, k).start()
-
-                    side_copy(way, step, k).start()
-
             for way in range(2):
                 if way % half == k:
                     @pl.when(step > 1)
@@ -226,6 +215,17 @@
                                 copy.wait()
 
                     work(way, step - 1)
+
+            @pl.when(step < chips)
+            def _():
+                for way in range(2):
+                    ring_wait(way, step, k)
+
+                    @pl.when(step < chips - 1)
+                    def _():
+                        ring_copy(way, step + 1, k).start()
+
+                    side_copy(way, step, k).start()
         return carry
 
     lax.fori_loop(1, chips + 1, turn, 0)
@@ -433,7 +433,6 @@
     half = orbs // 2
     sibling = me + 1 - 2 * core
     ends = (dev(place + 1, core), dev(place - 1, core))
-    greet([ends[0], ends[1], sibling])
     chunk = 32
 
     def position(way, step):
@@ -447,17 +446,24 @@
         r = dev(position(way, step), 1 - core) * orbs + way * half + k
         return remote(terms_ref.at[r], side.at[way, step, k], side_send.at[way, step, k], side_recv.at[way, step, k], sibling)
 
-    def load(step):
+    def load_own(step):
+        for k in range(half):
+            for way in range(2):
+                own_copy(way, step, k).start()
+
+    def load_side(step):
         for k in range(half):
             for way in range(2):
                 side_copy(way, step, k).start()
-                own_copy(way, step, k).start()
 
     def ring_copy(way, step, k):
         return remote(side.at[way, step, k], got.at[way, step, k], ring_send.at[way, step, k], ring_recv.at[way, step, k], ends[way])
 
-    load(0)
-    load(1)
+    load_own(0)
+    load_own(1)
+    greet([ends[0], ends[1], sibling])
+    load_side(0)
+    load_side(1)
     for step in range(chips):
         for k in range(half):
             for way in range(2):
@@ -480,7 +486,8 @@
                 if step < chips - 1:
                     ring_copy(way, step, k).start()
         if step + 2 < chips:
-            load(step + 2)
+            load_side(step + 2)
+            load_own(step + 2)
     for step in range(chips):
         for k in range(half):
             for way in range(2):

time: 235 us -> 236 us (level)
  no operation moved by 1% of the time
where the time goes in v5:
time: 236 us; the launch traced here: 233 us
  Pallas kernels  224 us (95%)
  other arithmetic  5.78 us (2%)
  local copies, waits for them, and re-layouts  3.09 us (1%)
    pallas_call x1, Pallas kernels, gather(): pl.pallas_call(functools.partial(gather_kernel, n, per_owner), name='gath...  104 us
    pallas_call x1, Pallas kernels, home(): pl.pallas_call(functools.partial(home_kernel, n), name='terms_home', out_...  88.6 us
    pallas_call x1, Pallas kernels, density_call(): pl.pallas_call(functools.partial(density_kernel, group), name='density_te...  30.6 us

profile of v5, /device:TPU:15, one launch (start us, length us, event | category | flops | bytes accessed | tf_op | source)
XLA Modules:
  0.0 233.2 jit_solution(16866121485434004986)
XLA Ops:
  0.6 0.7 fusion.4
  1.3 0.7 select_reduce_fusion.1.second_s
  2.0 0.0 copy-start
  2.0 0.1 fusion.1
  2.1 0.6 convert_element_type.14.seen_s
  2.7 0.9 convert_reduce_fusion
  3.6 0.7 multiply_add_fusion.row_s
  4.3 0.0 copy-start.1
  4.3 0.6 select_reduce_fusion.row_s
  4.9 0.9 fusion
  5.8 0.6 convert_subtract_fusion
  6.4 104.4 %gather_coulomb.1 = (bf16[96,200,512]{2,1,0:T(8,128)(2,1)}, bf16[96,200,512]{2,1,0:T(8,128)(2,1)}, f32[96,200,200]{2,1,0:T(8,128)}, f32[8,128]{1,0:T(8,128)}) custom-call(s32[48]{0:T(128)} %first_s.3, s32[32]{0:T(128)} %fetch_s.1, s32[96]{0:T(128)} %select_reduce_fusion.row_s, f32[4]{0:T(128)} %occ_s.1, bf16[4,256,512]{2,1,0:T(8,128)(2,1)} %x_ref.1, ...), custom_call_target="tpu_custom_call" | custom-call | tf_op jit(solution)/shard_map/gather_coulomb/pallas_call | solution.py:272
  110.8 0.0 copy-done
  110.9 0.0 copy-done.1
  110.9 30.6 %density_terms.1 = (f32[48,200,200]{2,1,0:T(8,128)}, f32[4,256,512]{2,1,0:T(8,128)}, bf16[64,256,512]{2,1,0:T(8,128)(2,1)}) custom-call(s32[48]{0:T(128)} %first_s.3, s32[48]{0:T(128)} %bitcast.5, s32[48]{0:T(128)} %copy-done, s32[48]{0:T(128)} %get-tuple-element.19.fresh_s, s32[48]{0:T(128)} %get-tuple-element.18.final_s, s32[64]{0:T(128)} %convert_element_type.14.seen_s, ...), custom_call_target="tpu_custom_call" | custom-call | tf_op jit(solution)/shard_map/density_terms/pallas_call | solution.py:397
  141.4 88.6 %terms_home.1 = f32[4,256,512]{2,1,0:T(8,128)} custom-call(bf16[64,256,512]{2,1,0:T(8,128)(2,1)} %get-tuple-element.14.terms_ref, f32[4,256,512]{2,1,0:T(8,128)} %get-tuple-element.15.dens_ref), custom_call_target="tpu_custom_call" | custom-call | tf_op jit(solution)/shard_map/terms_home/pallas_call | solution.py:504
  230.1 3.1 %copy.10 = f32[4,256,512]{2,1,0:T(8,128)} copy(f32[4,256,512]{2,1,0:T(8,128)} %terms_home.1) | data formatting | bytes 4194304
Async XLA Ops:
  2.0 108.8 %copy-start = (s32[48]{0:T(128)}, s32[48]{0:T(128)S(1)}, u32[]{:S(2)}) copy-start(s32[48]{0:T(128)S(1)} %select_reduce_fusion.1.second_s) | copy-start | bytes 580
  4.3 106.6 %copy-start.1 = (s32[48]{0:T(128)}, s32[48]{0:T(128)S(1)}, u32[]{:S(2)}) copy-start(s32[48]{0:T(128)S(1)} %multiply_add_fusion.row_s) | copy-start | bytes 580
